TPU v7x, 32 devices: a whole 2x2x4 slice. The times are simulated.
32 devices in a mesh: lon: 8 (over y, x, core), lat: 4 (over z).
Axes of the slice: x: 2, y: 2, z: 4, core: 2. Of those that a mesh axis runs over, the one named last changes fastest.
Arguments:
- tokens: bfloat16 [96, 32, 1024], P('lon', 'lat'), may hold values from -6 to 6
- query_local: bfloat16 [96, 32, 1024], P('lon', 'lat'), may hold values from -21 to 21, as said below
- key_local: bfloat16 [96, 32, 1024], P('lon', 'lat'), may hold values from -21 to 21, as said below
- value_local: bfloat16 [96, 32, 1024], P('lon', 'lat'), may hold values from -6 to 6
- position_bias: float32 [16, 13, 13], replicated, may hold values from -4 to 4
- output_weight: bfloat16 [1024, 1024], P('lat'), may hold values from -0.1875 to 0.1875
- norm_gain: float32 [1024], replicated, may hold values from 0.1 to 1.9
- global_weight: bfloat16 [1024, 3072], P('lat'), may hold values from -1 to 1
Outputs:
- hidden: bfloat16 [96, 32, 1024], P('lon', 'lat')
- attended: bfloat16 [96, 32, 1024], P('lon', 'lat')
Inputs may be any that keep to these rules, and one draw needn't show every extreme that they name: `query_local`: entries of the neighbourhood queries and keys. `key_local`: entries of the neighbourhood queries and keys.
All inputs are finite; a program needn't handle non-finite values.
Results may differ from a plain program's by a relative error of at most 0.015.
Values may be sent and summed in bfloat16 or wider, within the bound.
A program may use at most 64 MiB of HBM per device.

v0:
```python
import math

import jax
import jax.numpy as jnp
from jax import lax
from jax.sharding import PartitionSpec as P

STEPS = 4


def extended(block, sides, width):
    for axis, dim in sides:
        count = lax.axis_size(axis)
        forward = [(i, i + 1) for i in range(count - 1)]
        forward.append((count - 1, 0))
        backward = [(target, source) for source, target in forward]
        low = lax.ppermute(
            lax.slice_in_dim(block, block.shape[dim] - width, None, axis=dim), axis, forward
        )
        high = lax.ppermute(lax.slice_in_dim(block, 0, width, axis=dim), axis, backward)
        block = jnp.concatenate([low, block, high], axis=dim)
    return block


def from_behind(x, axis, by):
    count = lax.axis_size(axis)
    return lax.ppermute(x, axis, [(i, (i + by) % count) for i in range(count)])


def offset_table(cells, span, window):
    query_pos = lax.broadcasted_iota(jnp.int32, (cells, span, window), 0)
    key_pos = lax.broadcasted_iota(jnp.int32, (cells, span, window), 1)
    offset = lax.broadcasted_iota(jnp.int32, (cells, span, window), 2)
    return (key_pos - query_pos == offset).astype(jnp.float32)


def fold_rows(left, weight_rows):
    return jnp.dot(left, weight_rows, preferred_element_type=jnp.float32)


def block_merge(carry_state, query_heads, key_block, score_scale):
    running_max, denominator, accumulated = carry_state
    head_count = query_heads.shape[1]
    head_size = query_heads.shape[2]
    keys_part = key_block[0].reshape(key_block.shape[1], head_count, head_size)
    values_part = key_block[1].reshape(key_block.shape[1], head_count, head_size)
    scores = (
        jnp.einsum("qhd,khd->hqk", query_heads, keys_part, preferred_element_type=jnp.float32)
        * score_scale
    )
    new_max = jnp.maximum(running_max, jnp.max(scores, axis=2))
    factor = jnp.exp(running_max - new_max)
    weights = jnp.exp(scores - new_max[:, :, None])
    denominator = denominator * factor + jnp.sum(weights, axis=2)
    weighted = jnp.einsum(
        "hqk,khd->hqd",
        weights.astype(jnp.bfloat16),
        values_part,
        preferred_element_type=jnp.float32,
    )
    accumulated = accumulated * factor[:, :, None] + weighted
    return (new_max, denominator, accumulated)


def body(
    tokens,
    query_local,
    key_local,
    value_local,
    position_bias,
    output_weight,
    norm_gain,
    global_weight,
):
    lon_cells, lat_cells, model_width = tokens.shape
    head_count = position_bias.shape[0]
    radius = (position_bias.shape[1] - 1) // 2
    window = 2 * radius + 1
    head_size = model_width // head_count
    score_scale = 1.0 / math.sqrt(head_size)
    token_count = lon_cells * lat_cells
    lon_span = lon_cells + 2 * radius
    lat_span = lat_cells + 2 * radius
    stacked = jnp.stack([key_local, value_local])
    padded = extended(stacked, (("lon", 1), ("lat", 2)), radius)
    window_keys = padded[0].reshape(lon_span * lat_span, head_count, head_size)
    window_values = padded[1].reshape(lon_span * lat_span, head_count, head_size)
    query_heads = query_local.reshape(token_count, head_count, head_size)
    lon_table = offset_table(lon_cells, lon_span, window)
    lat_table = offset_table(lat_cells, lat_span, window)
    lat_start = lax.axis_index("lat") * lat_cells
    lat_total = lat_cells * lax.axis_size("lat")
    lat_global = lat_start + jnp.arange(lat_span, dtype=jnp.int32) - radius
    lat_inside = (lat_global >= 0) & (lat_global < lat_total)
    lon_near = jnp.sum(lon_table, axis=2) > 0.5
    lat_near = (jnp.sum(lat_table, axis=2) > 0.5) & lat_inside[None, :]
    allowed = (lon_near[:, None, :, None] & lat_near[None, :, None, :]).reshape(
        token_count, lon_span * lat_span
    )

    def one_head(operands):
        query_one, key_one, value_one, bias_one = operands
        bias_lat = jnp.einsum("ab,jkb->ajk", bias_one, lat_table, precision=lax.Precision.HIGHEST)
        bias_full = jnp.einsum(
            "ajk,ila->ijlk", bias_lat, lon_table, precision=lax.Precision.HIGHEST
        )
        bias_full = bias_full.reshape(token_count, lon_span * lat_span)
        scores = jnp.einsum("qd,kd->qk", query_one, key_one, preferred_element_type=jnp.float32)
        scores = jnp.where(allowed, scores * score_scale + bias_full, -1e30)
        largest = jnp.max(scores, axis=1, keepdims=True)
        weights = jnp.exp(scores - largest)
        denominator = jnp.sum(weights, axis=1, keepdims=True)
        weighted = jnp.dot(
            weights.astype(jnp.bfloat16), value_one, preferred_element_type=jnp.float32
        )
        return (weighted / denominator).astype(jnp.bfloat16)

    head_outputs = lax.map(
        one_head,
        (
            jnp.transpose(query_heads, (1, 0, 2)),
            jnp.transpose(window_keys, (1, 0, 2)),
            jnp.transpose(window_values, (1, 0, 2)),
            position_bias,
        ),
    )
    local_out = jnp.transpose(head_outputs, (1, 0, 2)).reshape(token_count, model_width)
    flat_tokens = tokens.reshape(token_count, model_width)
    projected = fold_rows(local_out, lax.all_gather(output_weight, "lat", axis=0, tiled=True))
    hidden = (flat_tokens.astype(jnp.float32) + projected).astype(jnp.bfloat16)
    widened_hidden = hidden.astype(jnp.float32)
    inverse = lax.rsqrt(jnp.mean(widened_hidden * widened_hidden, axis=1, keepdims=True) + 1e-06)
    normed = (widened_hidden * inverse * norm_gain).astype(jnp.bfloat16)
    triple = fold_rows(normed, lax.all_gather(global_weight, "lat", axis=0, tiled=True))
    triple = triple.astype(jnp.bfloat16)
    global_query = triple[:, :model_width].reshape(token_count, head_count, head_size)
    key_pair = jnp.stack([triple[:, model_width : 2 * model_width], triple[:, 2 * model_width :]])
    carry_state = (
        jnp.full((head_count, token_count), -1e30, jnp.float32),
        jnp.zeros((head_count, token_count), jnp.float32),
        jnp.zeros((head_count, token_count, head_size), jnp.float32),
    )
    carry_state = block_merge(carry_state, global_query, key_pair, score_scale)
    travelling = key_pair
    for hop_index in range(STEPS):
        travelling = from_behind(travelling, ("lon", "lat"), 1)
        carry_state = block_merge(carry_state, global_query, travelling, score_scale)
    running_max, denominator, accumulated = carry_state
    attended = accumulated / denominator[:, :, None]
    attended = (
        jnp.transpose(attended, (1, 0, 2))
        .reshape(lon_cells, lat_cells, model_width)
        .astype(jnp.bfloat16)
    )
    return (hidden.reshape(lon_cells, lat_cells, model_width), attended)


def solution(mesh):
    return jax.shard_map(
        body,
        mesh=mesh,
        in_specs=(
            P("lon", "lat", None),
            P("lon", "lat", None),
            P("lon", "lat", None),
            P("lon", "lat", None),
            P(),
            P("lat", None),
            P(),
            P("lat", None),
        ),
        out_specs=(P("lon", "lat", None), P("lon", "lat", None)),
        check_vma=False,
    )
```

profile of v0, /device:TPU:0, one launch (start us, length us, event | category | flops | bytes accessed | tf_op | source)
XLA Modules:
  0.0 273.7 jit_solution(18356017436903318245)
XLA Ops:
  9.8 2.9 %collective-permute-start.1 = (bf16[2,6,8,1024]{3,1,2,0:T(8,128)(2,1)S(1)}, bf16[2,6,8,1024]{3,1,2,0:T(8,128)(2,1)S(1)}, u32[]{:S(2)}, u32[]{:S(2)}) collective-permute-start(bf16[2,6,8,1024]{3,1,2,0:T(8,128)(2,1)S(1)} %get-tuple-element.134), channel_id=1, source_target_pairs={{4,0},{8,4},{12,8},{16,12},{20,16},{24,20},{28,24},{0,28},{5,1},{9... | collective-permute-start | bytes 589832 | tf_op jit(solution)/shard_map/ppermute | solution.py:20
  12.8 4.1 %collective-permute-done = bf16[2,6,8,1024]{3,1,2,0:T(8,128)(2,1)S(1)} collective-permute-done((bf16[2,6,8,1024]{3,1,2,0:T(8,128)(2,1)S(1)}, bf16[2,6,8,1024]{3,1,2,0:T(8,128)(2,1)S(1)}, u32[]{:S(2)}, u32[]{:S(2)}) %collective-permute-start) | collective-permute-done | bytes 196640 | tf_op jit(solution)/shard_map/ppermute | solution.py:17
  16.9 1.5 collective-permute-done.1
  19.8 1.6 collective-permute-start.2
  21.4 2.2 collective-permute-start.3
  24.2 25.8 %collective-permute-done.2 = bf16[2,24,6,1024]{3,1,2,0:T(8,128)(2,1)S(1)} collective-permute-done((bf16[2,24,6,1024]{3,1,2,0:T(8,128)(2,1)}, bf16[2,24,6,1024]{3,1,2,0:T(8,128)(2,1)S(1)}, u32[]{:S(2)}, u32[]{:S(2)}) %collective-permute-start.2) | collective-permute-done | bytes 589856 | tf_op jit(solution)/shard_map/ppermute | solution.py:17
  50.0 25.1 %collective-permute-done.3 = bf16[2,24,6,1024]{3,1,2,0:T(8,128)(2,1)} collective-permute-done((bf16[2,24,6,1024]{3,1,2,0:T(8,128)(2,1)S(1)}, bf16[2,24,6,1024]{3,1,2,0:T(8,128)(2,1)}, u32[]{:S(2)}, u32[]{:S(2)}) %collective-permute-start.3) | collective-permute-done | bytes 589856 | tf_op jit(solution)/shard_map/ppermute | solution.py:20
  75.2 1.6 pad_maximum_fusion
  78.4 1.3 reshape_squeeze.30
  79.8 1.8 copy.86
  82.2 1.3 reshape_squeeze.31
  83.5 1.8 copy.88
  85.3 103.0 %while.11 = (s32[]{:T(128)}, bf16[16,96,64]{1,2,0:T(8,128)(2,1)S(1)}, bf16[16,96,64]{2,1,0:T(8,128)(2,1)S(1)}, bf16[16,480,64]{2,1,0:T(8,128)(2,1)}, f32[16,13,1...) while((s32[]{:T(128)}, ...), condition=%wide.region_5.6_spmd.clone, body=%wide.region_2.5_spmd.clone.sunk | while | flops 19753728 | bytes 2181005 | solution.py:118
  188.4 2.2 fusion.48
  190.6 8.6 %all-gather.5.cloned.1.call-done = bf16[1024,3072]{1,0:T(8,128)(2,1)} async-done(((bf16[256,3072]{1,0:T(8,128)(2,1)}), bf16[1024,3072]{1,0:T(8,128)(2,1)}) %all-gather.5.cloned.1.call-update) | async-done | bytes 6291472 | tf_op jit(solution)/shard_map/all_gather | solution.py:134
  199.2 4.0 %convolution_convert_fusion = bf16[96,3072]{1,0:T(8,128)(2,1)S(1)} fusion(bf16[1024,3072]{1,0:T(8,128)(2,1)} %all-gather.5.cloned.1.call-done, bf16[96,1024]{1,0:T(8,128)(2,1)S(1)} %get-tuple-element.147, f32[1024]{0:T(1024)S(1)} %copy-done.10, f32[96]{0:T(128)S(1)} %add_rsqrt_fusion), kind=kOutput, calls=%fused_computation.32 | convolution fusion | flops 604667904 | bytes 7082368 | tf_op jit(solution)/shard_map/dot_general | solution.py:38
  204.9 13.2 %collective-permute-done.4 = bf16[2,96,1024]{2,1,0:T(8,128)(2,1)S(1)} collective-permute-done((bf16[2,96,1024]{2,1,0:T(8,128)(2,1)S(1)}, bf16[2,96,1024]{2,1,0:T(8,128)(2,1)S(1)}, u32[]{:S(2)}, u32[]{:S(2)}) %collective-permute-start.4) | collective-permute-done | bytes 393248 | tf_op jit(solution)/shard_map/ppermute | solution.py:27
  219.6 12.5 %collective-permute-done.5 = bf16[2,96,1024]{2,1,0:T(8,128)(2,1)} collective-permute-done((bf16[2,96,1024]{2,1,0:T(8,128)(2,1)S(1)}, bf16[2,96,1024]{2,1,0:T(8,128)(2,1)}, u32[]{:S(2)}, u32[]{:S(2)}) %collective-permute-start.5) | collective-permute-done | bytes 393248 | tf_op jit(solution)/shard_map/ppermute | solution.py:27
  234.4 10.1 %collective-permute-done.6 = bf16[2,96,1024]{2,1,0:T(8,128)(2,1)} collective-permute-done((bf16[2,96,1024]{2,1,0:T(8,128)(2,1)}, bf16[2,96,1024]{2,1,0:T(8,128)(2,1)}, u32[]{:S(2)}, u32[]{:S(2)}) %collective-permute-start.6) | collective-permute-done | bytes 393248 | tf_op jit(solution)/shard_map/ppermute | solution.py:27
  247.3 1.3 fusion.85
  248.6 7.1 %collective-permute-done.7 = bf16[2,96,1024]{2,1,0:T(8,128)(2,1)} collective-permute-done((bf16[2,96,1024]{2,1,0:T(8,128)(2,1)}, bf16[2,96,1024]{2,1,0:T(8,128)(2,1)}, u32[]{:S(2)}, u32[]{:S(2)}) %collective-permute-start.7) | collective-permute-done | bytes 393248 | tf_op jit(solution)/shard_map/ppermute | solution.py:27
  255.7 1.8 fusion.80
  257.5 1.8 copy.102
  259.2 2.1 fusion.84
  (240 shorter events, 122.4 us)
Async XLA Ops:
  7.2 181.2 %all-gather.3.cloned.1.call-start = ((), (), s32[]{:S(2)}) async-start(), calls=%async_computation | async-start | bytes 2621440 | tf_op jit(solution)/shard_map/all_gather | solution.py:129
  7.9 191.3 %all-gather.5.cloned.1.call-start = ((), (), s32[]{:S(2)}) async-start(), calls=%async_computation.1 | async-start | bytes 7864320 | tf_op jit(solution)/shard_map/all_gather | solution.py:134
  9.3 7.6 %collective-permute-start = (bf16[2,6,8,1024]{3,1,2,0:T(8,128)(2,1)S(1)}, bf16[2,6,8,1024]{3,1,2,0:T(8,128)(2,1)S(1)}, u32[]{:S(2)}, u32[]{:S(2)}) collective-permute-start(bf16[2,6,8,1024]{3,1,2,0:T(8,128)(2,1)S(1)} %get-tuple-element.133), channel_id=1, source_target_pairs={{0,4},{4,8},{8,12},{12,16},{16,20},{20,24},{24,28},{28,0},{1,5},{5... | collective-permute-start | bytes 589832 | tf_op jit(solution)/shard_map/ppermute | solution.py:17
  9.8 8.6 %collective-permute-start.1 = (bf16[2,6,8,1024]{3,1,2,0:T(8,128)(2,1)S(1)}, bf16[2,6,8,1024]{3,1,2,0:T(8,128)(2,1)S(1)}, u32[]{:S(2)}, u32[]{:S(2)}) collective-permute-start(bf16[2,6,8,1024]{3,1,2,0:T(8,128)(2,1)S(1)} %get-tuple-element.134), channel_id=1, source_target_pairs={{4,0},{8,4},{12,8},{16,12},{20,16},{24,20},{28,24},{0,28},{5,1},{9... | collective-permute-start | bytes 589832 | tf_op jit(solution)/shard_map/ppermute | solution.py:20
  18.8 4.9 %copy-start.9 = (bf16[12,8,1024]{2,1,0:T(8,128)(2,1)S(1)}, bf16[12,8,1024]{2,1,0:T(8,128)(2,1)}, u32[]{:S(2)}) copy-start(bf16[12,8,1024]{2,1,0:T(8,128)(2,1)} %param.11) | copy-start | bytes 589828
  19.8 30.2 %collective-permute-start.2 = (bf16[2,24,6,1024]{3,1,2,0:T(8,128)(2,1)}, bf16[2,24,6,1024]{3,1,2,0:T(8,128)(2,1)S(1)}, u32[]{:S(2)}, u32[]{:S(2)}) collective-permute-start(bf16[2,24,6,1024]{3,1,2,0:T(8,128)(2,1)} %get-tuple-element.126), channel_id=1, source_target_pairs={{0,1},{1,2},{2,3},{3,0},{4,5},{5,6},{6,7},{7,4},{8,9},{9,10},{10,1... | collective-permute-start | bytes 1769480 | tf_op jit(solution)/shard_map/ppermute | solution.py:17
  21.4 53.8 %collective-permute-start.3 = (bf16[2,24,6,1024]{3,1,2,0:T(8,128)(2,1)S(1)}, bf16[2,24,6,1024]{3,1,2,0:T(8,128)(2,1)}, u32[]{:S(2)}, u32[]{:S(2)}) collective-permute-start(bf16[2,24,6,1024]{3,1,2,0:T(8,128)(2,1)S(1)} %get-tuple-element.127), channel_id=1, source_target_pairs={{1,0},{2,1},{3,2},{0,3},{5,4},{6,5},{7,6},{4,7},{9,8},{10,9},{11,1... | collective-permute-start | bytes 1769480 | tf_op jit(solution)/shard_map/ppermute | solution.py:20
  79.8 1.9 copy-start
  83.5 1.8 copy-start.7
  85.3 103.1 %copy-start.8 = (bf16[12,8,1024]{2,1,0:T(8,128)(2,1)S(1)}, bf16[12,8,1024]{2,1,0:T(8,128)(2,1)}, u32[]{:S(2)}) copy-start(bf16[12,8,1024]{2,1,0:T(8,128)(2,1)} %param.10) | copy-start | bytes 589828
  188.3 10.9 %copy-start.10 = (f32[1024]{0:T(1024)S(1)}, f32[1024]{0:T(1024)}, u32[]{:S(2)}) copy-start(f32[1024]{0:T(1024)} %param.16) | copy-start | bytes 12292
  190.6 12.6 %copy-start.6 = (bf16[96,1024]{1,0:T(8,128)(2,1)}, bf16[96,1024]{1,0:T(8,128)(2,1)S(1)}, u32[]{:S(2)}) copy-start(bf16[96,1024]{1,0:T(8,128)(2,1)S(1)} %get-tuple-element.147) | copy-start | bytes 589828
  203.3 14.8 %collective-permute-start.4 = (bf16[2,96,1024]{2,1,0:T(8,128)(2,1)S(1)}, bf16[2,96,1024]{2,1,0:T(8,128)(2,1)S(1)}, u32[]{:S(2)}, u32[]{:S(2)}) collective-permute-start(bf16[2,96,1024]{2,1,0:T(8,128)(2,1)S(1)} %pad_maximum_fusion.2), channel_id=1, source_target_pairs={{0,1},{1,2},{2,3},{3,4},{4,5},{5,6},{6,7},{7,8},{8,9},{9,10},{10,1... | collective-permute-start | bytes 1179656 | tf_op jit(solution)/shard_map/ppermute | solution.py:27
  218.2 13.9 %collective-permute-start.5 = (bf16[2,96,1024]{2,1,0:T(8,128)(2,1)S(1)}, bf16[2,96,1024]{2,1,0:T(8,128)(2,1)}, u32[]{:S(2)}, u32[]{:S(2)}) collective-permute-start(bf16[2,96,1024]{2,1,0:T(8,128)(2,1)S(1)} %collective-permute-done.4), channel_id=1, source_target_pairs={{0,1},{1,2},{2,3},{3,4},{4,5},{5,6},{6,7},{7,8},{8,9},{9,10},{10,1... | collective-permute-start | bytes 1179656 | tf_op jit(solution)/shard_map/ppermute | solution.py:27
  232.0 12.5 %collective-permute-start.6 = (bf16[2,96,1024]{2,1,0:T(8,128)(2,1)}, bf16[2,96,1024]{2,1,0:T(8,128)(2,1)}, u32[]{:S(2)}, u32[]{:S(2)}) collective-permute-start(bf16[2,96,1024]{2,1,0:T(8,128)(2,1)} %collective-permute-done.5), channel_id=1, source_target_pairs={{0,1},{1,2},{2,3},{3,4},{4,5},{5,6},{6,7},{7,8},{8,9},{9,10},{10,1... | collective-permute-start | bytes 1179656 | tf_op jit(solution)/shard_map/ppermute | solution.py:27
  244.6 11.1 %collective-permute-start.7 = (bf16[2,96,1024]{2,1,0:T(8,128)(2,1)}, bf16[2,96,1024]{2,1,0:T(8,128)(2,1)}, u32[]{:S(2)}, u32[]{:S(2)}) collective-permute-start(bf16[2,96,1024]{2,1,0:T(8,128)(2,1)} %collective-permute-done.6), channel_id=1, source_target_pairs={{0,1},{1,2},{2,3},{3,4},{4,5},{5,6},{6,7},{7,8},{8,9},{9,10},{10,1... | collective-permute-start | bytes 1179656 | tf_op jit(solution)/shard_map/ppermute | solution.py:27
  262.5 1.1 copy-start.1
  262.5 1.3 copy-start.2
  262.8 1.3 copy-start.3
  263.8 1.0 copy-start.4
  264.1 1.0 copy-start.5
Sparse Core Ops, SparseCore 0:
  9.6 73.6 all-gather.2
  84.9 114.2 all-gather.4
where the time goes:
time: 276 us; the launch traced here: 274 us
  waiting for transfers between devices  109 us (39%)
  matrix products  71.2 us (26%)
  local copies, waits for them, and re-layouts  61.4 us (22%)
  between operations  14.5 us (5%)
  other arithmetic  9.46 us (3%)
  starting transfers between devices  7.42 us (3%)
    ppermute x4, waiting for transfers between devices, from_behind(): return lax.ppermute(x, axis, [(i, (i + by) % count) for i in range(count)])  42.9 us
    ppermute x2, waiting for transfers between devices, extended(): lax.ppermute(lax.slice_in_dim(block, block.shape[dim] - width, None, axis...  29.9 us
    ppermute x2, waiting for transfers between devices, extended(): lax.ppermute(lax.slice_in_dim(block, 0, width, axis=dim), axis, backward)  26.7 us
    dot_general x16, matrix products, one_head(): jnp.einsum('qd,kd->qk', query_one, key_one, preferred_element_type=jnp.fl...  19.4 us
    dot_general x16, matrix products, one_head(): jnp.dot(weights.astype(jnp.bfloat16), value_one, preferred_element_type=j...  18.6 us
    dot_general x16, matrix products, one_head(): jnp.einsum('ajk,ila->ijlk', bias_lat, lon_table, precision=lax.Precision....  18.3 us
    dynamic_slice x16, local copies, waits for them, and re-layouts, body(): lax.map(one_head, (jnp.transpose(query_heads, (1, 0, 2)), jnp.transpose(w...  13.2 us
    transpose x16, local copies, waits for them, and re-layouts, one_head(): jnp.einsum('ajk,ila->ijlk', bias_lat, lon_table, precision=lax.Precision....  10.1 us
  transfers between devices with their start and end apart: 10, of which 9 were waited for; matrix products, arithmetic and copies ran while one was open for 46% of the time, Pallas kernels for 0%

commit v1 on v0

v1 whole, which is shorter than its diff:
```python
import functools

import jax
import jax.numpy as jnp
from jax import lax
from jax.experimental import pallas as pl
from jax.experimental.pallas import tpu as pltpu
from jax.sharding import PartitionSpec as P

STEPS = 4
CHUNKS = 4
NEG = -1e30
MESH = pl.DeviceIdType.MESH


def kernel(
    n_lon,
    n_lat,
    pieces,
    tok_ref,
    q_ref,
    k_hbm,
    v_hbm,
    b_ref,
    wo_hbm,
    gain_ref,
    wg_hbm,
    hid_ref,
    att_ref,
    kbuf,
    vbuf,
    wo,
    wg,
    rbuf,
    lo,
    nbuf,
    gq,
    gk,
    gv,
    own_sem,
    lat_s,
    lat_r,
    lon_s,
    lon_r,
    w1_s,
    w1_r,
    wp_s,
    wp_r,
    wa_s,
    wa_r,
    wb_s,
    wb_r,
    ex_s,
    ex_r,
):
    i = lax.axis_index("lon")
    z = lax.axis_index("lat")
    rows = wo_hbm.shape[0]
    part = rows // pieces
    tokens, width = tok_ref.shape
    half = tokens // 2
    seg = 2 * tokens
    cw = width // CHUNKS
    j = lax.rem(i, pieces)
    base = i - j
    mate = base + j + 1 - 2 * lax.rem(j, 2)
    hops = pieces // 2 - 1
    p = i * n_lat + z
    total = n_lon * n_lat

    def lat_dev(d):
        return (i, lax.rem(z + d + n_lat, n_lat))

    def lon_dev(d):
        return (lax.rem(i + d + n_lon, n_lon), z)

    def peer(k):
        return base + lax.rem(j + 2 * k + pieces, pieces)

    def line_dev(s):
        t = lax.rem(p + s + total, total)
        return (t // n_lat, lax.rem(t, n_lat))

    def rc(src, dst, ssem, rsem, dev):
        return pltpu.make_async_remote_copy(
            src_ref=src, dst_ref=dst, send_sem=ssem, recv_sem=rsem, device_id=dev, device_id_type=MESH
        )

    barrier = pltpu.get_barrier_semaphore()
    greet = [lat_dev(-d) for d in range(1, n_lat)]
    greet += [lon_dev(1), lon_dev(-1), (mate, z)]
    greet += [(peer(-k), z) for k in range(1, hops + 1)]
    greet += [line_dev(-s) for s in range(1, STEPS + 1)]
    for dev in greet:
        pl.semaphore_signal(barrier, inc=1, device_id=dev, device_id_type=MESH)

    pairs = ((k_hbm, kbuf), (v_hbm, vbuf))
    weights = ((wo_hbm, wo), (wg_hbm, wg))
    own_copies = []
    for a, (src, dst) in enumerate(pairs):
        own_copies.append(
            pltpu.make_async_copy(src, dst.at[pl.ds(seg + half, tokens)], own_sem.at[a])
        )
    for a, (src, dst) in enumerate(weights):
        own_copies.append(
            pltpu.make_async_copy(
                src, dst.at[pl.ds(pl.multiple_of(z * rows, 16), rows)], own_sem.at[2 + a]
            )
        )
    for copy in own_copies:
        copy.start()
    pl.semaphore_wait(barrier, len(greet))

    def cols(c):
        return pl.ds(c * cw, cw)

    def lat_copy(a, way, c):
        src, dst = pairs[a]
        at = 0 if way == 0 else 2
        return rc(
            src.at[:, cols(c)],
            dst.at[pl.ds(at * seg + half, tokens), cols(c)],
            lat_s.at[a, way, c],
            lat_r.at[a, way, c],
            lat_dev(1 if way == 0 else -1),
        )

    def lon_copy(a, s, way, c):
        src, dst = pairs[a]
        if s == 1:
            source = src.at[pl.ds(half if way == 0 else 0, half), cols(c)]
        else:
            source = dst.at[pl.ds(s * seg + (tokens if way == 0 else half), half), cols(c)]
        return rc(
            source,
            dst.at[pl.ds(s * seg + (0 if way == 0 else half + tokens), half), cols(c)],
            lon_s.at[a, s, way, c],
            lon_r.at[a, s, way, c],
            lon_dev(1 if way == 0 else -1),
        )

    has_up = z < n_lat - 1
    has_down = z > 0

    for c in range(CHUNKS):
        @pl.when(has_up)
        def _():
            for a in range(2):
                lat_copy(a, 0, c).start()

        @pl.when(has_down)
        def _():
            for a in range(2):
                lat_copy(a, 1, c).start()

        for a in range(2):
            for way in range(2):
                lon_copy(a, 1, way, c).start()

    def w_rows(shard, piece):
        return pl.ds(pl.multiple_of(shard * rows + piece * part, 16), part)

    def w1_copy(a, d):
        src, dst = weights[a]
        return rc(
            src.at[pl.ds(pl.multiple_of(j * part, 16), part)],
            dst.at[w_rows(z, j)],
            w1_s.at[a, d],
            w1_r.at[a, d],
            lat_dev(d),
        )

    def w_move(a, d, piece, ssem, rsem, dev):
        ref = weights[a][1].at[w_rows(lax.rem(z - d + n_lat, n_lat), piece)]
        return rc(ref, ref, ssem, rsem, dev)

    def w1_wait(a, d):
        w_move(a, d, j, w1_s.at[a, d], w1_r.at[a, d], lat_dev(d)).wait_recv()

    def wp_copy(a, d, piece):
        return w_move(a, d, piece, wp_s.at[a, d], wp_r.at[a, d], (mate, z))

    def wa_copy(a, d, k, piece):
        return w_move(a, d, piece, wa_s.at[a, d, k], wa_r.at[a, d, k], (peer(k), z))

    def wb_copy(a, d, k, piece):
        return w_move(a, d, piece, wb_s.at[a, d, k], wb_r.at[a, d, k], (mate, z))

    mate_piece = mate - base

    def far_piece(k):
        return lax.rem(j - 2 * k + pieces, pieces)

    def mate_far_piece(k):
        return lax.rem(mate_piece - 2 * k + pieces, pieces)

    def spread(a):
        for d in range(1, n_lat):
            w1_wait(a, d)
            wp_copy(a, d, j).start()
            for k in range(1, hops + 1):
                wa_copy(a, d, k, j).start()

    def relay(a):
        for d in range(1, n_lat):
            for k in range(1, hops + 1):
                wa_copy(a, d, k, far_piece(k)).wait_recv()
                wb_copy(a, d, k, far_piece(k)).start()

    def gathered(a):
        own_copies[2 + a].wait()
        for d in range(1, n_lat):
            wp_copy(a, d, mate_piece).wait_recv()
            for k in range(1, hops + 1):
                wb_copy(a, d, k, mate_far_piece(k)).wait_recv()

    for a in range(2):
        for d in range(1, n_lat):
            w1_copy(a, d).start()

    pad_rows = kbuf.shape[0] - 3 * seg
    for ref in (kbuf, vbuf):
        ref[pl.ds(3 * seg, pad_rows), :] = jnp.zeros((pad_rows, width), jnp.bfloat16)

        @pl.when(jnp.logical_not(has_down))
        def _():
            ref[pl.ds(0, seg), :] = jnp.zeros((seg, width), jnp.bfloat16)

        @pl.when(jnp.logical_not(has_up))
        def _():
            ref[pl.ds(2 * seg, seg), :] = jnp.zeros((seg, width), jnp.bfloat16)

    for ref in (gk, gv):
        pad = ref.shape[0] - (STEPS + 1) * tokens
        ref[pl.ds((STEPS + 1) * tokens, pad), :] = jnp.zeros((pad, width), jnp.bfloat16)

    lanes = kbuf.shape[0]
    flat = b_ref[...]
    row_id = lax.broadcasted_iota(jnp.int32, flat.shape, 0)
    shifted = jnp.zeros_like(flat)
    for r in range(8):
        shifted = jnp.where(lax.rem(row_id, 8) == r, pltpu.roll(flat, r + 2, 1), shifted)
    lane = lax.broadcasted_iota(jnp.int32, (flat.shape[1], lanes), 1)
    spot = lax.broadcasted_iota(jnp.int32, (flat.shape[1], lanes), 0)
    at_seg = (lane >= seg).astype(jnp.int32) + (lane >= 2 * seg).astype(jnp.int32)
    inner = lane - at_seg * seg
    wanted = lax.shift_right_logical(inner, 3) * 24 + at_seg * 8 + (inner & 7)
    pick = jnp.where(spot == wanted, 1.0, 0.0).astype(jnp.bfloat16)
    first = shifted.astype(jnp.bfloat16)
    rest = shifted - first.astype(jnp.float32)
    second = rest.astype(jnp.bfloat16)
    third = (rest - second.astype(jnp.float32)).astype(jnp.bfloat16)
    bias = jnp.dot(first, pick, preferred_element_type=jnp.float32)
    bias = bias + jnp.dot(second, pick, preferred_element_type=jnp.float32)
    bias = bias + jnp.dot(third, pick, preferred_element_type=jnp.float32)
    lane = lax.broadcasted_iota(jnp.int32, bias.shape, 1)
    jrow = lax.rem(lax.broadcasted_iota(jnp.int32, bias.shape, 0), 8)
    at_seg = (lane >= seg).astype(jnp.int32) + (lane >= 2 * seg).astype(jnp.int32)
    inner = lane - at_seg * seg
    index = at_seg * 8 + (inner & 7) - jrow - 2
    low_lane = jnp.where(has_down, 0, seg)
    high_lane = jnp.where(has_up, 3 * seg, 2 * seg)
    fits = (inner < 13 * 8) & (index >= 0) & (index < 13) & (lane >= low_lane) & (lane < high_lane)
    rbuf[...] = jnp.where(fits, bias, NEG)

    def forward(c):
        @pl.when(has_down)
        def _():
            for a in range(2):
                lat_copy(a, 0, c).wait_recv()
                for way in range(2):
                    lon_copy(a, 0, way, c).start()

        @pl.when(has_up)
        def _():
            for a in range(2):
                lat_copy(a, 1, c).wait_recv()
                for way in range(2):
                    lon_copy(a, 2, way, c).start()

    def landed(c):
        for a in range(2):
            for way in range(2):
                lon_copy(a, 1, way, c).wait_recv()

        @pl.when(has_down)
        def _():
            for a in range(2):
                for way in range(2):
                    lon_copy(a, 0, way, c).wait_recv()

        @pl.when(has_up)
        def _():
            for a in range(2):
                for way in range(2):
                    lon_copy(a, 2, way, c).wait_recv()

    left = (lax.broadcasted_iota(jnp.int32, (tokens, 128), 1) < 64).astype(jnp.float32)
    left_mask = left.astype(jnp.bfloat16)
    right_mask = (1.0 - left).astype(jnp.bfloat16)

    def two_heads(q2, k2, v2, fix):
        qq = jnp.concatenate([q2 * left_mask, q2 * right_mask], axis=0)
        s = lax.dot_general(qq, k2, (((1,), (1,)), ((), ())), preferred_element_type=jnp.float32)
        s = fix(s * 0.125)
        e = jnp.exp(s - jnp.max(s, axis=1, keepdims=True))
        t = jnp.sum(e, axis=1, keepdims=True)
        o = jnp.dot(e.astype(jnp.bfloat16), v2, preferred_element_type=jnp.float32) / t
        return jnp.where(left > 0.5, o[:tokens], o[tokens:]).astype(jnp.bfloat16)

    def local_pair(h):
        at = pl.ds(pl.multiple_of(h * 128, 128), 128)

        def fix(s):
            parts = []
            for head in range(2):
                r = rbuf[pl.ds(pl.multiple_of(h * 16 + head * 8, 8), 8), :]
                for col in range(tokens // 8):
                    parts.append(r if col == 0 else pltpu.roll(r, col * 8, 1))
            return s + jnp.concatenate(parts, axis=0)

        lo[:, at] = two_heads(q_ref[:, at], kbuf[:, at], vbuf[:, at], fix)

    per = cw // 128
    for c in range(CHUNKS):
        forward(c)
    spread(0)
    for copy in own_copies[:2]:
        copy.wait()
    for c in range(CHUNKS):
        landed(c)
        pl.loop(c * per, (c + 1) * per)(local_pair)
        if c == 0:
            spread(1)
        if c == CHUNKS - 2:
            relay(0)
    gathered(0)

    projected = jnp.dot(lo[...], wo[...], preferred_element_type=jnp.float32)
    hidden = (tok_ref[...].astype(jnp.float32) + projected).astype(jnp.bfloat16)
    hid_ref[...] = hidden
    wide = hidden.astype(jnp.float32)
    inverse = lax.rsqrt(jnp.mean(wide * wide, axis=1, keepdims=True) + 1e-06)
    nbuf[pl.ds(0, tokens), :] = (wide * inverse * gain_ref[...]).astype(jnp.bfloat16)

    def ex_copy(s):
        return rc(
            nbuf.at[pl.ds(0, tokens)],
            nbuf.at[pl.ds(s * tokens, tokens)],
            ex_s.at[s],
            ex_r.at[s],
            line_dev(s),
        )

    for s in range(1, STEPS + 1):
        ex_copy(s).start()
    relay(1)
    gathered(1)

    tile = 512

    def project(at, count, column):
        left_rows = nbuf[pl.ds(at, count), :]
        weight = wg[:, pl.ds(pl.multiple_of(column, tile), tile)]
        return jnp.dot(left_rows, weight, preferred_element_type=jnp.float32).astype(jnp.bfloat16)

    def keys_values(at, count):
        @pl.loop(0, width // tile)
        def _(t):
            here = pl.ds(pl.multiple_of(t * tile, tile), tile)
            gk[pl.ds(at, count), here] = project(at, count, width + t * tile)
            gv[pl.ds(at, count), here] = project(at, count, 2 * width + t * tile)

    @pl.loop(0, width // tile)
    def _(t):
        here = pl.ds(pl.multiple_of(t * tile, tile), tile)
        gq[:, here] = project(0, tokens, t * tile)

    keys_values(0, tokens)
    for s in range(1, STEPS + 1):
        ex_copy(s).wait_recv()
        if s % 2 == 0:
            keys_values((s - 1) * tokens, 2 * tokens)

    def global_pair(h):
        at = pl.ds(pl.multiple_of(h * 128, 128), 128)

        def fix(s):
            key = lax.broadcasted_iota(jnp.int32, s.shape, 1)
            return jnp.where(key < (STEPS + 1) * tokens, s, NEG)

        att_ref[:, at] = two_heads(gq[:, at], gk[:, at], gv[:, at], fix)

    pl.loop(0, width // 128)(global_pair)

    for c in range(CHUNKS):
        for a in range(2):
            for way in range(2):
                lon_copy(a, 1, way, c).wait_send()

        @pl.when(has_up)
        def _():
            for a in range(2):
                lat_copy(a, 0, c).wait_send()
                for way in range(2):
                    lon_copy(a, 2, way, c).wait_send()

        @pl.when(has_down)
        def _():
            for a in range(2):
                lat_copy(a, 1, c).wait_send()
                for way in range(2):
                    lon_copy(a, 0, way, c).wait_send()

    for a in range(2):
        for d in range(1, n_lat):
            w1_copy(a, d).wait_send()
            wp_copy(a, d, j).wait_send()
            for k in range(1, hops + 1):
                wa_copy(a, d, k, j).wait_send()
                wb_copy(a, d, k, far_piece(k)).wait_send()
    for s in range(1, STEPS + 1):
        ex_copy(s).wait_send()


def body(tokens, query_local, key_local, value_local, position_bias, output_weight, norm_gain, global_weight):
    n_lon = lax.axis_size("lon")
    n_lat = lax.axis_size("lat")
    lon_cells, lat_cells, width = tokens.shape
    count = lon_cells * lat_cells
    heads, window, _ = position_bias.shape
    rows = output_weight.shape[0]
    pieces = min(n_lon, rows // 16)
    hops = pieces // 2

    def flat(x):
        return x.reshape(count, width)

    table = jnp.pad(position_bias, ((0, 0), (0, 0), (0, 24 - window))).reshape(heads, window * 24)
    table = jnp.pad(table, ((0, 0), (0, 384 - window * 24)))
    table = jnp.broadcast_to(table[:, None, :], (heads, 8, 384)).reshape(heads * 8, 384)
    lanes = -(-(6 * count) // 128) * 128
    keys = -(-((STEPS + 1) * count) // 128) * 128
    vmem = pl.BlockSpec(memory_space=pltpu.VMEM)
    hbm = pl.BlockSpec(memory_space=pl.ANY)
    dma = pltpu.SemaphoreType.DMA
    bf16 = jnp.bfloat16
    hidden, attended = pl.pallas_call(
        functools.partial(kernel, n_lon, n_lat, pieces),
        out_shape=(jax.ShapeDtypeStruct((count, width), bf16),) * 2,
        in_specs=[vmem, vmem, hbm, hbm, vmem, hbm, vmem, hbm],
        out_specs=(vmem, vmem),
        scratch_shapes=[
            pltpu.VMEM((lanes, width), bf16),
            pltpu.VMEM((lanes, width), bf16),
            pltpu.VMEM((width, width), bf16),
            pltpu.VMEM((width, 3 * width), bf16),
            pltpu.VMEM((heads * 8, lanes), jnp.float32),
            pltpu.VMEM((count, width), bf16),
            pltpu.VMEM(((STEPS + 1) * count, width), bf16),
            pltpu.VMEM((count, width), bf16),
            pltpu.VMEM((keys, width), bf16),
            pltpu.VMEM((keys, width), bf16),
            dma((4,)),
            dma((2, 2, CHUNKS)),
            dma((2, 2, CHUNKS)),
            dma((2, 3, 2, CHUNKS)),
            dma((2, 3, 2, CHUNKS)),
            dma((2, n_lat)),
            dma((2, n_lat)),
            dma((2, n_lat)),
            dma((2, n_lat)),
            dma((2, n_lat, hops)),
            dma((2, n_lat, hops)),
            dma((2, n_lat, hops)),
            dma((2, n_lat, hops)),
            dma((STEPS + 1,)),
            dma((STEPS + 1,)),
        ],
        compiler_params=pltpu.CompilerParams(
            collective_id=0, has_side_effects=True, vmem_limit_bytes=48 * 1024 * 1024
        ),
    )(
        flat(tokens),
        flat(query_local),
        flat(key_local),
        flat(value_local),
        table,
        output_weight,
        norm_gain.reshape(1, width),
        global_weight,
    )
    return hidden.reshape(tokens.shape), attended.reshape(tokens.shape)


def solution(mesh):
    return jax.shard_map(
        body,
        mesh=mesh,
        in_specs=(
            P("lon", "lat", None),
            P("lon", "lat", None),
            P("lon", "lat", None),
            P("lon", "lat", None),
            P(),
            P("lat", None),
            P(),
            P("lat", None),
        ),
        out_specs=(P("lon", "lat", None), P("lon", "lat", None)),
        check_vma=False,
    )
```

time: 276 us -> 84.4 us (0.31)
  the two profiles are of different devices: /device:TPU:0 before, /device:TPU:1 now
where the time goes in v1:
time: 84.4 us; the launch traced here: 84 us
  Pallas kernels  74.1 us (88%)
  local copies, waits for them, and re-layouts  9.27 us (11%)
    pallas_call x1, Pallas kernels, body(): pl.pallas_call(functools.partial(kernel, n_lon, n_lat, pieces), out_shape...  74.1 us
    unnamed x17, local copies, waits for them, and re-layouts  9.13 us

profile of v1, /device:TPU:1, one launch (start us, length us, event | category | flops | bytes accessed | tf_op | source)
XLA Modules:
  0.0 84.0 jit_solution(13756905278975226429)
XLA Ops:
  0.6 0.9 %copy.11 = f32[16,13,13]{2,1,0:T(8,128)S(1)} copy(f32[16,13,13]{2,0,1:T(8,128)} %param.12) | data formatting | bytes 21632
  1.6 0.1 reshape.36
  1.7 0.0 copy-start
  1.7 1.4 %copy-done = bf16[256,3072]{1,0:T(8,128)(2,1)S(1)} copy-done((bf16[256,3072]{1,0:T(8,128)(2,1)S(1)}, bf16[256,3072]{1,0:T(8,128)(2,1)}, u32[]{:S(2)}) %copy-start) | copy-done | bytes 1572888
  3.1 0.0 copy-start.1
  3.1 1.0 %copy-done.1 = bf16[256,1024]{1,0:T(8,128)(2,1)S(1)} copy-done((bf16[256,1024]{1,0:T(8,128)(2,1)S(1)}, bf16[256,1024]{1,0:T(8,128)(2,1)}, u32[]{:S(2)}) %copy-start.1) | copy-done | bytes 524312
  4.2 0.0 copy-start.2
  4.2 0.9 %copy-done.2 = bf16[12,8,1024]{2,1,0:T(8,128)(2,1)S(1)} copy-done((bf16[12,8,1024]{2,1,0:T(8,128)(2,1)S(1)}, bf16[12,8,1024]{2,1,0:T(8,128)(2,1)}, u32[]{:S(2)}) %copy-start.2) | copy-done | bytes 196632
  5.1 0.0 copy-start.3
  5.1 0.9 %copy-done.3 = bf16[12,8,1024]{2,1,0:T(8,128)(2,1)S(1)} copy-done((bf16[12,8,1024]{2,1,0:T(8,128)(2,1)S(1)}, bf16[12,8,1024]{2,1,0:T(8,128)(2,1)}, u32[]{:S(2)}) %copy-start.3) | copy-done | bytes 196632
  6.0 0.0 copy-start.4
  6.0 0.9 %copy-done.4 = bf16[12,8,1024]{2,1,0:T(8,128)(2,1)S(1)} copy-done((bf16[12,8,1024]{2,1,0:T(8,128)(2,1)S(1)}, bf16[12,8,1024]{2,1,0:T(8,128)(2,1)}, u32[]{:S(2)}) %copy-start.4) | copy-done | bytes 196632
  7.0 0.0 copy-start.5
  7.0 0.9 %copy-done.5 = bf16[12,8,1024]{2,1,0:T(8,128)(2,1)S(1)} copy-done((bf16[12,8,1024]{2,1,0:T(8,128)(2,1)S(1)}, bf16[12,8,1024]{2,1,0:T(8,128)(2,1)}, u32[]{:S(2)}) %copy-start.5) | copy-done | bytes 196632
  7.9 0.0 copy-start.6
  7.9 0.7 copy-done.6
  8.6 74.1 %shard_map.95 = (bf16[96,1024]{1,0:T(8,128)(2,1)S(1)}, bf16[96,1024]{1,0:T(8,128)(2,1)S(1)}) custom-call(bf16[96,1024]{1,0:T(8,128)(2,1)S(1)} %bitcast.9, bf16[96,1024]{1,0:T(8,128)(2,1)S(1)} %bitcast.10, bf16[96,1024]{1,0:T(8,128)(2,1)S(1)} %bitcast.11, bf16[96,1024]{1,0:T(8,128)(2,1)S(1)} %bitcast.12, f32[128,384]{1,0:T(8,128)S(1)} %broadcast_bitcast_fusion.b_ref, ...), custom_call_target="tpu_custom_call" | custom-call | tf_op jit(solution)/shard_map/pallas_call | solution.py:448
  82.7 0.7 copy.14
  83.4 0.7 copy.15
  (3 shorter events, 0.0 us)
Async XLA Ops:
  1.7 1.4 %copy-start = (bf16[256,3072]{1,0:T(8,128)(2,1)S(1)}, bf16[256,3072]{1,0:T(8,128)(2,1)}, u32[]{:S(2)}) copy-start(bf16[256,3072]{1,0:T(8,128)(2,1)} %wg_hbm.1) | copy-start | bytes 4718596
  3.1 1.0 %copy-start.1 = (bf16[256,1024]{1,0:T(8,128)(2,1)S(1)}, bf16[256,1024]{1,0:T(8,128)(2,1)}, u32[]{:S(2)}) copy-start(bf16[256,1024]{1,0:T(8,128)(2,1)} %wo_hbm.1) | copy-start | bytes 1572868
  4.2 0.9 %copy-start.2 = (bf16[12,8,1024]{2,1,0:T(8,128)(2,1)S(1)}, bf16[12,8,1024]{2,1,0:T(8,128)(2,1)}, u32[]{:S(2)}) copy-start(bf16[12,8,1024]{2,1,0:T(8,128)(2,1)} %param.8) | copy-start | bytes 589828
  5.1 0.9 %copy-start.3 = (bf16[12,8,1024]{2,1,0:T(8,128)(2,1)S(1)}, bf16[12,8,1024]{2,1,0:T(8,128)(2,1)}, u32[]{:S(2)}) copy-start(bf16[12,8,1024]{2,1,0:T(8,128)(2,1)} %param.9) | copy-start | bytes 589828
  6.0 0.9 %copy-start.4 = (bf16[12,8,1024]{2,1,0:T(8,128)(2,1)S(1)}, bf16[12,8,1024]{2,1,0:T(8,128)(2,1)}, u32[]{:S(2)}) copy-start(bf16[12,8,1024]{2,1,0:T(8,128)(2,1)} %param.10) | copy-start | bytes 589828
  7.0 0.9 %copy-start.5 = (bf16[12,8,1024]{2,1,0:T(8,128)(2,1)S(1)}, bf16[12,8,1024]{2,1,0:T(8,128)(2,1)}, u32[]{:S(2)}) copy-start(bf16[12,8,1024]{2,1,0:T(8,128)(2,1)} %param.11) | copy-start | bytes 589828
  7.9 0.7 copy-start.6

commit v2 on v1

--- a/solution.py
+++ b/solution.py
@@ -17,16 +17,20 @@
     n_lon,
     n_lat,
     pieces,
-    tok_ref,
-    q_ref,
+    tok_hbm,
+    q_hbm,
     k_hbm,
     v_hbm,
-    b_ref,
+    b_hbm,
     wo_hbm,
-    gain_ref,
+    gain_hbm,
     wg_hbm,
     hid_ref,
     att_ref,
+    tok_ref,
+    q_ref,
+    b_ref,
+    gain_ref,
     kbuf,
     vbuf,
     wo,
@@ -46,10 +50,12 @@
     w1_r,
     wp_s,
     wp_r,
-    wa_s,
-    wa_r,
-    wb_s,
-    wb_r,
+    wx_s,
+    wx_r,
+    wh_s,
+    wh_r,
+    wm_s,
+    wm_r,
     ex_s,
     ex_r,
 ):
@@ -63,8 +69,12 @@
     cw = width // CHUNKS
     j = lax.rem(i, pieces)
     base = i - j
-    mate = base + j + 1 - 2 * lax.rem(j, 2)
-    hops = pieces // 2 - 1
+    dims = pieces.bit_length() - 2
+
+    def flip(at, bit):
+        return at + bit - 2 * bit * lax.rem(at // bit, 2)
+
+    mate = base + flip(j, 1)
     p = i * n_lat + z
     total = n_lon * n_lat
 
@@ -74,8 +84,8 @@
     def lon_dev(d):
         return (lax.rem(i + d + n_lon, n_lon), z)
 
-    def peer(k):
-        return base + lax.rem(j + 2 * k + pieces, pieces)
+    def side(e):
+        return (base + flip(j, 2 << e), z)
 
     def line_dev(s):
         t = lax.rem(p + s + total, total)
@@ -89,7 +99,7 @@
     barrier = pltpu.get_barrier_semaphore()
     greet = [lat_dev(-d) for d in range(1, n_lat)]
     greet += [lon_dev(1), lon_dev(-1), (mate, z)]
-    greet += [(peer(-k), z) for k in range(1, hops + 1)]
+    greet += [side(e) for e in range(dims)]
     greet += [line_dev(-s) for s in range(1, STEPS + 1)]
     for dev in greet:
         pl.semaphore_signal(barrier, inc=1, device_id=dev, device_id_type=MESH)
@@ -107,8 +117,11 @@
                 src, dst.at[pl.ds(pl.multiple_of(z * rows, 16), rows)], own_sem.at[2 + a]
             )
         )
-    for copy in own_copies:
-        copy.start()
+    singles = ((b_hbm, b_ref), (q_hbm, q_ref), (tok_hbm, tok_ref), (gain_hbm, gain_ref))
+    for a, (src, dst) in enumerate(singles):
+        own_copies.append(pltpu.make_async_copy(src, dst, own_sem.at[4 + a]))
+    for at in (4, 0, 1, 5, 2, 3, 6, 7):
+        own_copies[at].start()
     pl.semaphore_wait(barrier, len(greet))
 
     def cols(c):
@@ -142,21 +155,6 @@
     has_up = z < n_lat - 1
     has_down = z > 0
 
-    for c in range(CHUNKS):
-        @pl.when(has_up)
-        def _():
-            for a in range(2):
-                lat_copy(a, 0, c).start()
-
-        @pl.when(has_down)
-        def _():
-            for a in range(2):
-                lat_copy(a, 1, c).start()
-
-        for a in range(2):
-            for way in range(2):
-                lon_copy(a, 1, way, c).start()
-
     def w_rows(shard, piece):
         return pl.ds(pl.multiple_of(shard * rows + piece * part, 16), part)
 
@@ -180,43 +178,83 @@
     def wp_copy(a, d, piece):
         return w_move(a, d, piece, wp_s.at[a, d], wp_r.at[a, d], (mate, z))
 
-    def wa_copy(a, d, k, piece):
-        return w_move(a, d, piece, wa_s.at[a, d, k], wa_r.at[a, d, k], (peer(k), z))
-
-    def wb_copy(a, d, k, piece):
-        return w_move(a, d, piece, wb_s.at[a, d, k], wb_r.at[a, d, k], (mate, z))
-
-    mate_piece = mate - base
-
-    def far_piece(k):
-        return lax.rem(j - 2 * k + pieces, pieces)
-
-    def mate_far_piece(k):
-        return lax.rem(mate_piece - 2 * k + pieces, pieces)
-
-    def spread(a):
-        for d in range(1, n_lat):
+    def w_half(a, d, piece, e, ssem, rsem, dev):
+        size = part // 2
+        at = lax.rem(z - d + n_lat, n_lat) * rows + piece * part + e * size
+        ref = weights[a][1].at[pl.ds(pl.multiple_of(at, 16), size)]
+        return rc(ref, ref, ssem, rsem, dev)
+
+    def wx_copy(a, d, e, piece):
+        return w_move(a, d, piece, wx_s.at[a, d, e], wx_r.at[a, d, e], side(e))
+
+    def wh_copy(a, d, e, piece):
+        return w_half(a, d, piece, e, wh_s.at[a, d, e], wh_r.at[a, d, e], side(1 - e))
+
+    def wm_copy(a, d, e, piece):
+        return w_move(a, d, piece, wm_s.at[a, d, e], wm_r.at[a, d, e], (mate, z))
+
+    mate_piece = flip(j, 1)
+    corners = 1 if dims == 2 else 0
+
+    def across(at, e):
+        return flip(at, 2 << e) if e < 2 else flip(flip(at, 2), 4)
+
+    def spread(a, ds):
+        for d in ds:
             w1_wait(a, d)
+            for e in range(dims):
+                wx_copy(a, d, e, j).start()
             wp_copy(a, d, j).start()
-            for k in range(1, hops + 1):
-                wa_copy(a, d, k, j).start()
-
-    def relay(a):
-        for d in range(1, n_lat):
-            for k in range(1, hops + 1):
-                wa_copy(a, d, k, far_piece(k)).wait_recv()
-                wb_copy(a, d, k, far_piece(k)).start()
+
+    def relay(a, ds):
+        for d in ds:
+            for e in range(dims):
+                piece = across(j, e)
+                wx_copy(a, d, e, piece).wait_recv()
+                if corners:
+                    wh_copy(a, d, e, piece).start()
+                wm_copy(a, d, e, piece).start()
+
+    def corner(a, ds):
+        if corners:
+            for d in ds:
+                piece = across(j, 2)
+                for e in range(2):
+                    wh_copy(a, d, e, piece).wait_recv()
+                wm_copy(a, d, 2, piece).start()
 
     def gathered(a):
         own_copies[2 + a].wait()
-        for d in range(1, n_lat):
+        for d in near:
             wp_copy(a, d, mate_piece).wait_recv()
-            for k in range(1, hops + 1):
-                wb_copy(a, d, k, mate_far_piece(k)).wait_recv()
-
-    for a in range(2):
-        for d in range(1, n_lat):
-            w1_copy(a, d).start()
+            for e in range(dims + corners):
+                wm_copy(a, d, e, across(mate_piece, e)).wait_recv()
+
+    near = sorted(range(1, n_lat), key=lambda d: min(d, n_lat - d))
+    third = len(near) // 3
+    thirds = (near[:third], near[third : 2 * third], near[2 * third :])
+
+    for c in range(CHUNKS):
+        @pl.when(has_up)
+        def _():
+            for a in range(2):
+                lat_copy(a, 0, c).start()
+
+        @pl.when(has_down)
+        def _():
+            for a in range(2):
+                lat_copy(a, 1, c).start()
+
+        for a in range(2):
+            for way in range(2):
+                lon_copy(a, 1, way, c).start()
+
+        if c == 0:
+            for d in near:
+                w1_copy(0, d).start()
+        else:
+            for d in thirds[c - 1]:
+                w1_copy(1, d).start()
 
     pad_rows = kbuf.shape[0] - 3 * seg
     for ref in (kbuf, vbuf):
@@ -235,6 +273,7 @@
         ref[pl.ds((STEPS + 1) * tokens, pad), :] = jnp.zeros((pad, width), jnp.bfloat16)
 
     lanes = kbuf.shape[0]
+    own_copies[4].wait()
     flat = b_ref[...]
     row_id = lax.broadcasted_iota(jnp.int32, flat.shape, 0)
     shifted = jnp.zeros_like(flat)
@@ -322,18 +361,27 @@
         lo[:, at] = two_heads(q_ref[:, at], kbuf[:, at], vbuf[:, at], fix)
 
     per = cw // 128
-    for c in range(CHUNKS):
-        forward(c)
-    spread(0)
+    forward(0)
+    spread(0, near)
+    forward(1)
+    spread(1, thirds[0])
+    own_copies[5].wait()
     for copy in own_copies[:2]:
         copy.wait()
     for c in range(CHUNKS):
         landed(c)
         pl.loop(c * per, (c + 1) * per)(local_pair)
+        if c < 2:
+            forward(c + 2)
+            spread(1, thirds[c + 1])
         if c == 0:
-            spread(1)
-        if c == CHUNKS - 2:
-            relay(0)
+            relay(0, near)
+        if c == 1:
+            corner(0, near)
+        if c > 1:
+            relay(1, thirds[c - 2])
+    own_copies[6].wait()
+    own_copies[7].wait()
     gathered(0)
 
     projected = jnp.dot(lo[...], wo[...], preferred_element_type=jnp.float32)
@@ -354,7 +402,9 @@
 
     for s in range(1, STEPS + 1):
         ex_copy(s).start()
-    relay(1)
+    relay(1, thirds[2])
+    for some in thirds:
+        corner(1, some)
     gathered(1)
 
     tile = 512
@@ -376,11 +426,9 @@
         here = pl.ds(pl.multiple_of(t * tile, tile), tile)
         gq[:, here] = project(0, tokens, t * tile)
 
-    keys_values(0, tokens)
     for s in range(1, STEPS + 1):
         ex_copy(s).wait_recv()
-        if s % 2 == 0:
-            keys_values((s - 1) * tokens, 2 * tokens)
+    keys_values(0, (STEPS + 1) * tokens)
 
     def global_pair(h):
         at = pl.ds(pl.multiple_of(h * 128, 128), 128)
@@ -416,9 +464,12 @@
         for d in range(1, n_lat):
             w1_copy(a, d).wait_send()
             wp_copy(a, d, j).wait_send()
-            for k in range(1, hops + 1):
-                wa_copy(a, d, k, j).wait_send()
-                wb_copy(a, d, k, far_piece(k)).wait_send()
+            for e in range(dims):
+                wx_copy(a, d, e, j).wait_send()
+                if corners:
+                    wh_copy(a, d, e, across(j, e)).wait_send()
+            for e in range(dims + corners):
+                wm_copy(a, d, e, across(j, e)).wait_send()
     for s in range(1, STEPS + 1):
         ex_copy(s).wait_send()
 
@@ -430,8 +481,7 @@
     count = lon_cells * lat_cells
     heads, window, _ = position_bias.shape
     rows = output_weight.shape[0]
-    pieces = min(n_lon, rows // 16)
-    hops = pieces // 2
+    pieces = min(n_lon, 8 if rows >= 256 else 4)
 
     def flat(x):
         return x.reshape(count, width)
@@ -442,15 +492,19 @@
     lanes = -(-(6 * count) // 128) * 128
     keys = -(-((STEPS + 1) * count) // 128) * 128
     vmem = pl.BlockSpec(memory_space=pltpu.VMEM)
-    hbm = pl.BlockSpec(memory_space=pl.ANY)
+    hbm = pl.BlockSpec(memory_space=pltpu.HBM)
     dma = pltpu.SemaphoreType.DMA
     bf16 = jnp.bfloat16
     hidden, attended = pl.pallas_call(
         functools.partial(kernel, n_lon, n_lat, pieces),
         out_shape=(jax.ShapeDtypeStruct((count, width), bf16),) * 2,
-        in_specs=[vmem, vmem, hbm, hbm, vmem, hbm, vmem, hbm],
+        in_specs=[hbm] * 8,
         out_specs=(vmem, vmem),
         scratch_shapes=[
+            pltpu.VMEM((count, width), bf16),
+            pltpu.VMEM((count, width), bf16),
+            pltpu.VMEM((heads * 8, 384), jnp.float32),
+            pltpu.VMEM((1, width), jnp.float32),
             pltpu.VMEM((lanes, width), bf16),
             pltpu.VMEM((lanes, width), bf16),
             pltpu.VMEM((width, width), bf16),
@@ -461,7 +515,7 @@
             pltpu.VMEM((count, width), bf16),
             pltpu.VMEM((keys, width), bf16),
             pltpu.VMEM((keys, width), bf16),
-            dma((4,)),
+            dma((8,)),
             dma((2, 2, CHUNKS)),
             dma((2, 2, CHUNKS)),
             dma((2, 3, 2, CHUNKS)),
@@ -470,15 +524,17 @@
             dma((2, n_lat)),
             dma((2, n_lat)),
             dma((2, n_lat)),
-            dma((2, n_lat, hops)),
-            dma((2, n_lat, hops)),
-            dma((2, n_lat, hops)),
-            dma((2, n_lat, hops)),
+            dma((2, n_lat, 2)),
+            dma((2, n_lat, 2)),
+            dma((2, n_lat, 2)),
+            dma((2, n_lat, 2)),
+            dma((2, n_lat, 3)),
+            dma((2, n_lat, 3)),
             dma((STEPS + 1,)),
             dma((STEPS + 1,)),
         ],
         compiler_params=pltpu.CompilerParams(
-            collective_id=0, has_side_effects=True, vmem_limit_bytes=48 * 1024 * 1024
+            collective_id=0, has_side_effects=True, vmem_limit_bytes=60 * 1024 * 1024
         ),
     )(
         flat(tokens),

time: 84.4 us -> 75.5 us (0.89)
  the two profiles are of different devices: /device:TPU:1 before, /device:TPU:0 now
where the time goes in v2:
time: 75.5 us; the launch traced here: 75.3 us
  Pallas kernels  69.7 us (92%)
  local copies, waits for them, and re-layouts  4.98 us (7%)
    pallas_call x1, Pallas kernels, body(): pl.pallas_call(functools.partial(kernel, n_lon, n_lat, pieces), out_shape...  69.7 us
    unnamed x3, local copies, waits for them, and re-layouts  4.17 us

profile of v2, /device:TPU:0, one launch (start us, length us, event | category | flops | bytes accessed | tf_op | source)
XLA Modules:
  0.0 75.3 jit_solution(15971345370612553294)
XLA Ops:
  0.6 0.9 %copy.11 = f32[16,13,13]{2,1,0:T(8,128)S(1)} copy(f32[16,13,13]{2,0,1:T(8,128)} %param.12) | data formatting | bytes 21632
  1.6 0.1 reshape.36
  1.7 0.7 broadcast_bitcast_fusion.b_hbm
  2.4 69.7 %shard_map.95 = (bf16[96,1024]{1,0:T(8,128)(2,1)}, bf16[96,1024]{1,0:T(8,128)(2,1)}) custom-call(bf16[96,1024]{1,0:T(8,128)(2,1)} %bitcast.9, bf16[96,1024]{1,0:T(8,128)(2,1)} %bitcast.10, bf16[96,1024]{1,0:T(8,128)(2,1)} %bitcast.11, bf16[96,1024]{1,0:T(8,128)(2,1)} %bitcast.12, f32[128,384]{1,0:T(8,128)} %broadcast_bitcast_fusion.b_hbm, ...), custom_call_target="tpu_custom_call" | custom-call | tf_op jit(solution)/shard_map/pallas_call | solution.py:498
  72.1 1.6 %copy.14 = bf16[12,8,1024]{2,1,0:T(8,128)(2,1)} copy(bf16[12,8,1024]{2,1,0:T(8,128)(2,1)} %bitcast.14) | data formatting | bytes 393216
  73.7 1.6 %copy.15 = bf16[12,8,1024]{2,1,0:T(8,128)(2,1)} copy(bf16[12,8,1024]{2,1,0:T(8,128)(2,1)} %bitcast.13) | data formatting | bytes 393216
  (2 shorter events, 0.0 us)

commit v3 on v2

--- a/solution.py
+++ b/solution.py
@@ -97,7 +97,7 @@
         )
 
     barrier = pltpu.get_barrier_semaphore()
-    greet = [lat_dev(-d) for d in range(1, n_lat)]
+    greet = [lat_dev(1), lat_dev(-1)]
     greet += [lon_dev(1), lon_dev(-1), (mate, z)]
     greet += [side(e) for e in range(dims)]
     greet += [line_dev(-s) for s in range(1, STEPS + 1)]
@@ -155,43 +155,54 @@
     has_up = z < n_lat - 1
     has_down = z > 0
 
+    routes = [(way, d) for d in range(1, n_lat) for way in (1, -1)]
+
+    def shard_of(way, d):
+        return z - way * d
+
+    def exists(way, d):
+        return (shard_of(way, d) >= 0) & (shard_of(way, d) < n_lat)
+
     def w_rows(shard, piece):
         return pl.ds(pl.multiple_of(shard * rows + piece * part, 16), part)
 
-    def w1_copy(a, d):
+    def w_move(a, shard, piece, ssem, rsem, dev):
+        ref = weights[a][1].at[w_rows(shard, piece)]
+        return rc(ref, ref, ssem, rsem, dev)
+
+    def w1_copy(a, way, d):
+        shard = shard_of(way, d - 1)
+        sems = (w1_s.at[a, max(way, 0), d], w1_r.at[a, max(way, 0), d])
+        if d > 1:
+            return w_move(a, shard, j, *sems, lat_dev(way))
         src, dst = weights[a]
-        return rc(
-            src.at[pl.ds(pl.multiple_of(j * part, 16), part)],
-            dst.at[w_rows(z, j)],
-            w1_s.at[a, d],
-            w1_r.at[a, d],
-            lat_dev(d),
-        )
-
-    def w_move(a, d, piece, ssem, rsem, dev):
-        ref = weights[a][1].at[w_rows(lax.rem(z - d + n_lat, n_lat), piece)]
-        return rc(ref, ref, ssem, rsem, dev)
-
-    def w1_wait(a, d):
-        w_move(a, d, j, w1_s.at[a, d], w1_r.at[a, d], lat_dev(d)).wait_recv()
-
-    def wp_copy(a, d, piece):
-        return w_move(a, d, piece, wp_s.at[a, d], wp_r.at[a, d], (mate, z))
-
-    def w_half(a, d, piece, e, ssem, rsem, dev):
+        piece = src.at[pl.ds(pl.multiple_of(j * part, 16), part)]
+        return rc(piece, dst.at[w_rows(z, j)], *sems, lat_dev(way))
+
+    def w1_wait(a, way, d):
+        sems = (w1_s.at[a, max(way, 0), d], w1_r.at[a, max(way, 0), d])
+        w_move(a, shard_of(way, d), j, *sems, lat_dev(way)).wait_recv()
+
+    def onward(way, d):
+        return exists(way, d - 1) & (has_up if way > 0 else has_down)
+
+    def wp_copy(a, t, piece):
+        return w_move(a, t, piece, wp_s.at[a, t], wp_r.at[a, t], (mate, z))
+
+    def w_half(a, t, piece, e, ssem, rsem, dev):
         size = part // 2
-        at = lax.rem(z - d + n_lat, n_lat) * rows + piece * part + e * size
+        at = t * rows + piece * part + e * size
         ref = weights[a][1].at[pl.ds(pl.multiple_of(at, 16), size)]
         return rc(ref, ref, ssem, rsem, dev)
 
-    def wx_copy(a, d, e, piece):
-        return w_move(a, d, piece, wx_s.at[a, d, e], wx_r.at[a, d, e], side(e))
-
-    def wh_copy(a, d, e, piece):
-        return w_half(a, d, piece, e, wh_s.at[a, d, e], wh_r.at[a, d, e], side(1 - e))
-
-    def wm_copy(a, d, e, piece):
-        return w_move(a, d, piece, wm_s.at[a, d, e], wm_r.at[a, d, e], (mate, z))
+    def wx_copy(a, t, e, piece):
+        return w_move(a, t, piece, wx_s.at[a, t, e], wx_r.at[a, t, e], side(e))
+
+    def wh_copy(a, t, e, piece):
+        return w_half(a, t, piece, e, wh_s.at[a, t, e], wh_r.at[a, t, e], side(1 - e))
+
+    def wm_copy(a, t, e, piece):
+        return w_move(a, t, piece, wm_s.at[a, t, e], wm_r.at[a, t, e], (mate, z))
 
     mate_piece = flip(j, 1)
     corners = 1 if dims == 2 else 0
@@ -199,40 +210,57 @@
     def across(at, e):
         return flip(at, 2 << e) if e < 2 else flip(flip(at, 2), 4)
 
+    def each(ds, step):
+        for way, d in routes:
+            if d in ds:
+                pl.when(exists(way, d))(functools.partial(step, way, d))
+
     def spread(a, ds):
-        for d in ds:
-            w1_wait(a, d)
+        def step(way, d):
+            w1_wait(a, way, d)
+            if d + 1 < n_lat:
+                pl.when(onward(way, d + 1))(lambda: w1_copy(a, way, d + 1).start())
+            t = shard_of(way, d)
             for e in range(dims):
-                wx_copy(a, d, e, j).start()
-            wp_copy(a, d, j).start()
+                wx_copy(a, t, e, j).start()
+            wp_copy(a, t, j).start()
+
+        each(ds, step)
 
     def relay(a, ds):
-        for d in ds:
+        def step(way, d):
+            t = shard_of(way, d)
             for e in range(dims):
                 piece = across(j, e)
-                wx_copy(a, d, e, piece).wait_recv()
+                wx_copy(a, t, e, piece).wait_recv()
                 if corners:
-                    wh_copy(a, d, e, piece).start()
-                wm_copy(a, d, e, piece).start()
+                    wh_copy(a, t, e, piece).start()
+                wm_copy(a, t, e, piece).start()
+
+        each(ds, step)
 
     def corner(a, ds):
+        def step(way, d):
+            t = shard_of(way, d)
+            piece = across(j, 2)
+            for e in range(2):
+                wh_copy(a, t, e, piece).wait_recv()
+            wm_copy(a, t, 2, piece).start()
+
         if corners:
-            for d in ds:
-                piece = across(j, 2)
-                for e in range(2):
-                    wh_copy(a, d, e, piece).wait_recv()
-                wm_copy(a, d, 2, piece).start()
+            each(ds, step)
 
     def gathered(a):
+        def step(way, d):
+            t = shard_of(way, d)
+            wp_copy(a, t, mate_piece).wait_recv()
+            for e in range(dims + corners):
+                wm_copy(a, t, e, across(mate_piece, e)).wait_recv()
+
         own_copies[2 + a].wait()
-        for d in near:
-            wp_copy(a, d, mate_piece).wait_recv()
-            for e in range(dims + corners):
-                wm_copy(a, d, e, across(mate_piece, e)).wait_recv()
-
-    near = sorted(range(1, n_lat), key=lambda d: min(d, n_lat - d))
-    third = len(near) // 3
-    thirds = (near[:third], near[third : 2 * third], near[2 * third :])
+        each(range(1, n_lat), step)
+
+    one, two, three = (1,), (2,), tuple(range(3, n_lat))
 
     for c in range(CHUNKS):
         @pl.when(has_up)
@@ -249,12 +277,9 @@
             for way in range(2):
                 lon_copy(a, 1, way, c).start()
 
-        if c == 0:
-            for d in near:
-                w1_copy(0, d).start()
-        else:
-            for d in thirds[c - 1]:
-                w1_copy(1, d).start()
+    for a in range(2):
+        for way in (1, -1):
+            pl.when(onward(way, 1))(lambda: w1_copy(a, way, 1).start())
 
     pad_rows = kbuf.shape[0] - 3 * seg
     for ref in (kbuf, vbuf):
@@ -361,25 +386,28 @@
         lo[:, at] = two_heads(q_ref[:, at], kbuf[:, at], vbuf[:, at], fix)
 
     per = cw // 128
-    forward(0)
-    spread(0, near)
-    forward(1)
-    spread(1, thirds[0])
+    for c in range(CHUNKS):
+        forward(c)
+    spread(0, one)
     own_copies[5].wait()
     for copy in own_copies[:2]:
         copy.wait()
     for c in range(CHUNKS):
         landed(c)
         pl.loop(c * per, (c + 1) * per)(local_pair)
-        if c < 2:
-            forward(c + 2)
-            spread(1, thirds[c + 1])
         if c == 0:
-            relay(0, near)
+            spread(0, two)
+            relay(0, one)
         if c == 1:
-            corner(0, near)
-        if c > 1:
-            relay(1, thirds[c - 2])
+            spread(1, one)
+            spread(0, three)
+            relay(0, two)
+        if c == 2:
+            spread(1, two)
+            relay(0, three)
+            corner(0, one + two)
+    corner(0, three)
+    relay(1, one)
     own_copies[6].wait()
     own_copies[7].wait()
     gathered(0)
@@ -391,20 +419,37 @@
     inverse = lax.rsqrt(jnp.mean(wide * wide, axis=1, keepdims=True) + 1e-06)
     nbuf[pl.ds(0, tokens), :] = (wide * inverse * gain_ref[...]).astype(jnp.bfloat16)
 
+    def block(s):
+        return nbuf.at[pl.ds(s * tokens, tokens)]
+
     def ex_copy(s):
-        return rc(
-            nbuf.at[pl.ds(0, tokens)],
-            nbuf.at[pl.ds(s * tokens, tokens)],
-            ex_s.at[s],
-            ex_r.at[s],
-            line_dev(s),
-        )
-
-    for s in range(1, STEPS + 1):
-        ex_copy(s).start()
-    relay(1, thirds[2])
-    for some in thirds:
-        corner(1, some)
+        return rc(block(0), block(s), ex_s.at[s], ex_r.at[s], line_dev(s))
+
+    staged = n_lat == 4
+
+    def direct(s, act):
+        if staged and s == 3:
+            pl.when(z != 0)(act)
+        elif staged and s == 1:
+            pl.when(z != n_lat - 1)(act)
+        else:
+            act()
+
+    up_copy = rc(block(2), block(3), ex_s.at[0], ex_r.at[3], lat_dev(1))
+    down_copy = rc(block(2), block(1), ex_s.at[0], ex_r.at[1], lat_dev(-1))
+
+    for s in (2, 3, 1, 4):
+        direct(s, lambda: ex_copy(s).start())
+    spread(1, three)
+    relay(1, two)
+    corner(1, one)
+    ex_copy(2).wait_recv()
+    if staged:
+        pl.when(z == 2)(lambda: up_copy.start())
+        pl.when(z == 1)(lambda: down_copy.start())
+    relay(1, three)
+    corner(1, two)
+    corner(1, three)
     gathered(1)
 
     tile = 512
@@ -426,7 +471,7 @@
         here = pl.ds(pl.multiple_of(t * tile, tile), tile)
         gq[:, here] = project(0, tokens, t * tile)
 
-    for s in range(1, STEPS + 1):
+    for s in (1, 3, 4):
         ex_copy(s).wait_recv()
     keys_values(0, (STEPS + 1) * tokens)
 
@@ -461,17 +506,24 @@
                     lon_copy(a, 0, way, c).wait_send()
 
     for a in range(2):
-        for d in range(1, n_lat):
-            w1_copy(a, d).wait_send()
-            wp_copy(a, d, j).wait_send()
+        def sent(way, d):
+            t = shard_of(way, d)
+            wp_copy(a, t, j).wait_send()
             for e in range(dims):
-                wx_copy(a, d, e, j).wait_send()
+                wx_copy(a, t, e, j).wait_send()
                 if corners:
-                    wh_copy(a, d, e, across(j, e)).wait_send()
+                    wh_copy(a, t, e, across(j, e)).wait_send()
             for e in range(dims + corners):
-                wm_copy(a, d, e, across(j, e)).wait_send()
+                wm_copy(a, t, e, across(j, e)).wait_send()
+
+        each(range(1, n_lat), sent)
+        for way, d in routes:
+            pl.when(onward(way, d))(lambda: w1_copy(a, way, d).wait_send())
     for s in range(1, STEPS + 1):
-        ex_copy(s).wait_send()
+        direct(s, lambda: ex_copy(s).wait_send())
+    if staged:
+        pl.when(z == 2)(lambda: up_copy.wait_send())
+        pl.when(z == 1)(lambda: down_copy.wait_send())
 
 
 def body(tokens, query_local, key_local, value_local, position_bias, output_weight, norm_gain, global_weight):
@@ -520,8 +572,8 @@
             dma((2, 2, CHUNKS)),
             dma((2, 3, 2, CHUNKS)),
             dma((2, 3, 2, CHUNKS)),
-            dma((2, n_lat)),
-            dma((2, n_lat)),
+            dma((2, 2, n_lat)),
+            dma((2, 2, n_lat)),
             dma((2, n_lat)),
             dma((2, n_lat)),
             dma((2, n_lat, 2)),

time: 75.5 us -> 72.6 us (0.962)
  Pallas kernels: 69.7 us -> 66.8 us
    pallas_call x1, Pallas kernels: 69.7 us -> 66.8 us  [body(): pl.pallas_call(functools.partial(kernel, n_lon, n_lat, pieces), out_shape...]
where the time goes in v3:
time: 72.6 us; the launch traced here: 72.4 us
  Pallas kernels  66.8 us (92%)
  local copies, waits for them, and re-layouts  4.98 us (7%)
    pallas_call x1, Pallas kernels, body(): pl.pallas_call(functools.partial(kernel, n_lon, n_lat, pieces), out_shape...  66.8 us
    unnamed x3, local copies, waits for them, and re-layouts  4.17 us

profile of v3, /device:TPU:0, one launch (start us, length us, event | category | flops | bytes accessed | tf_op | source)
XLA Modules:
  0.0 72.4 jit_solution(7349149017695069913)
XLA Ops:
  0.6 0.9 %copy.11 = f32[16,13,13]{2,1,0:T(8,128)S(1)} copy(f32[16,13,13]{2,0,1:T(8,128)} %param.12) | data formatting | bytes 21632
  1.6 0.1 reshape.36
  1.7 0.7 broadcast_bitcast_fusion.b_hbm
  2.4 66.8 %shard_map.95 = (bf16[96,1024]{1,0:T(8,128)(2,1)}, bf16[96,1024]{1,0:T(8,128)(2,1)}) custom-call(bf16[96,1024]{1,0:T(8,128)(2,1)} %bitcast.9, bf16[96,1024]{1,0:T(8,128)(2,1)} %bitcast.10, bf16[96,1024]{1,0:T(8,128)(2,1)} %bitcast.11, bf16[96,1024]{1,0:T(8,128)(2,1)} %bitcast.12, f32[128,384]{1,0:T(8,128)} %broadcast_bitcast_fusion.b_hbm, ...), custom_call_target="tpu_custom_call" | custom-call | tf_op jit(solution)/shard_map/pallas_call | solution.py:550
  69.2 1.6 %copy.14 = bf16[12,8,1024]{2,1,0:T(8,128)(2,1)} copy(bf16[12,8,1024]{2,1,0:T(8,128)(2,1)} %bitcast.14) | data formatting | bytes 393216
  70.8 1.6 %copy.15 = bf16[12,8,1024]{2,1,0:T(8,128)(2,1)} copy(bf16[12,8,1024]{2,1,0:T(8,128)(2,1)} %bitcast.13) | data formatting | bytes 393216
  (2 shorter events, 0.0 us)

commit v4 on v3

--- a/solution.py
+++ b/solution.py
@@ -30,6 +30,7 @@
     tok_ref,
     q_ref,
     b_ref,
+    tab,
     gain_ref,
     kbuf,
     vbuf,
@@ -299,7 +300,14 @@
 
     lanes = kbuf.shape[0]
     own_copies[4].wait()
-    flat = b_ref[...]
+    window = b_ref.shape[0]
+    tab[...] = jnp.zeros_like(tab)
+    for r in range(window):
+        tab[:, r * 24 : r * 24 + window] = b_ref[r]
+    heads = tab.shape[0]
+    flat = jnp.concatenate(
+        [jnp.broadcast_to(tab[h : h + 1, :], (8, tab.shape[1])) for h in range(heads)], axis=0
+    )
     row_id = lax.broadcasted_iota(jnp.int32, flat.shape, 0)
     shifted = jnp.zeros_like(flat)
     for r in range(8):
@@ -364,9 +372,10 @@
     right_mask = (1.0 - left).astype(jnp.bfloat16)
 
     def two_heads(q2, k2, v2, fix):
+        q2 = q2 * jnp.bfloat16(0.125)
         qq = jnp.concatenate([q2 * left_mask, q2 * right_mask], axis=0)
         s = lax.dot_general(qq, k2, (((1,), (1,)), ((), ())), preferred_element_type=jnp.float32)
-        s = fix(s * 0.125)
+        s = fix(s)
         e = jnp.exp(s - jnp.max(s, axis=1, keepdims=True))
         t = jnp.sum(e, axis=1, keepdims=True)
         o = jnp.dot(e.astype(jnp.bfloat16), v2, preferred_element_type=jnp.float32) / t
@@ -386,26 +395,29 @@
         lo[:, at] = two_heads(q_ref[:, at], kbuf[:, at], vbuf[:, at], fix)
 
     per = cw // 128
-    for c in range(CHUNKS):
-        forward(c)
-    spread(0, one)
+    forward(0)
     own_copies[5].wait()
     for copy in own_copies[:2]:
         copy.wait()
+    forward(1)
+    forward(2)
     for c in range(CHUNKS):
         landed(c)
-        pl.loop(c * per, (c + 1) * per)(local_pair)
+        pl.loop(c * per, (c + 1) * per, unroll=per)(local_pair)
         if c == 0:
+            forward(3)
+            spread(0, one)
+        if c == 1:
             spread(0, two)
             relay(0, one)
-        if c == 1:
             spread(1, one)
+        if c == 2:
             spread(0, three)
             relay(0, two)
-        if c == 2:
             spread(1, two)
-            relay(0, three)
-            corner(0, one + two)
+            corner(0, one)
+    relay(0, three)
+    corner(0, two)
     corner(0, three)
     relay(1, one)
     own_copies[6].wait()
@@ -479,12 +491,15 @@
         at = pl.ds(pl.multiple_of(h * 128, 128), 128)
 
         def fix(s):
-            key = lax.broadcasted_iota(jnp.int32, s.shape, 1)
-            return jnp.where(key < (STEPS + 1) * tokens, s, NEG)
+            edge = s.shape[1] - 128
+            last = s[:, edge:]
+            key = lax.broadcasted_iota(jnp.int32, last.shape, 1)
+            last = jnp.where(key < (STEPS + 1) * tokens - edge, last, NEG)
+            return jnp.concatenate([s[:, :edge], last], axis=1)
 
         att_ref[:, at] = two_heads(gq[:, at], gk[:, at], gv[:, at], fix)
 
-    pl.loop(0, width // 128)(global_pair)
+    pl.loop(0, width // 128, unroll=4)(global_pair)
 
     for c in range(CHUNKS):
         for a in range(2):
@@ -538,9 +553,6 @@
     def flat(x):
         return x.reshape(count, width)
 
-    table = jnp.pad(position_bias, ((0, 0), (0, 0), (0, 24 - window))).reshape(heads, window * 24)
-    table = jnp.pad(table, ((0, 0), (0, 384 - window * 24)))
-    table = jnp.broadcast_to(table[:, None, :], (heads, 8, 384)).reshape(heads * 8, 384)
     lanes = -(-(6 * count) // 128) * 128
     keys = -(-((STEPS + 1) * count) // 128) * 128
     vmem = pl.BlockSpec(memory_space=pltpu.VMEM)
@@ -555,7 +567,8 @@
         scratch_shapes=[
             pltpu.VMEM((count, width), bf16),
             pltpu.VMEM((count, width), bf16),
-            pltpu.VMEM((heads * 8, 384), jnp.float32),
+            pltpu.VMEM((window, heads, window), jnp.float32),
+            pltpu.VMEM((heads, 384), jnp.float32),
             pltpu.VMEM((1, width), jnp.float32),
             pltpu.VMEM((lanes, width), bf16),
             pltpu.VMEM((lanes, width), bf16),
@@ -593,7 +606,7 @@
         flat(query_local),
         flat(key_local),
         flat(value_local),
-        table,
+        jnp.transpose(position_bias, (1, 0, 2)),
         output_weight,
         norm_gain.reshape(1, width),
         global_weight,

time: 72.6 us -> 69.5 us (0.957)
  local copies, waits for them, and re-layouts: 4.98 us -> 3.23 us
  Pallas kernels: 66.8 us -> 65.5 us
    pallas_call x1, Pallas kernels: 66.8 us -> 65.5 us  [body(): pl.pallas_call(functools.partial(kernel, n_lon, n_lat, pieces), out_shape...]
    unnamed x3 -> x2, local copies, waits for them, and re-layouts: 4.17 us -> 3.23 us
    reshape x2 -> x0, local copies, waits for them, and re-layouts: 0.79 us -> none  [the longest x1 0.69 us: body(): jnp.broadcast_to(table[:, None, :], (heads, 8, 384)).reshape(heads * 8, 384)]
where the time goes in v4:
time: 69.5 us; the launch traced here: 69.4 us
  Pallas kernels  65.5 us (94%)
  local copies, waits for them, and re-layouts  3.23 us (5%)
    pallas_call x1, Pallas kernels, body(): pl.pallas_call(functools.partial(kernel, n_lon, n_lat, pieces), out_shape...  65.5 us
    unnamed x2, local copies, waits for them, and re-layouts  3.23 us

profile of v4, /device:TPU:0, one launch (start us, length us, event | category | flops | bytes accessed | tf_op | source)
XLA Modules:
  0.0 69.4 jit_solution(12230475249973900499)
XLA Ops:
  0.6 65.5 %shard_map.95 = (bf16[96,1024]{1,0:T(8,128)(2,1)}, bf16[96,1024]{1,0:T(8,128)(2,1)}) custom-call(bf16[96,1024]{1,0:T(8,128)(2,1)} %bitcast.8, bf16[96,1024]{1,0:T(8,128)(2,1)} %bitcast.9, bf16[96,1024]{1,0:T(8,128)(2,1)} %bitcast.10, bf16[96,1024]{1,0:T(8,128)(2,1)} %bitcast.11, f32[13,16,13]{2,1,0:T(8,128)} %bitcast.14, bf16[256,1024]{1,0:T(8,128)(2,1)} %wo_hbm.1, ...), custom_call_target="tpu_custom_call" | custom-call | tf_op jit(solution)/shard_map/pallas_call | solution.py:562
  66.1 1.6 %copy.12 = bf16[12,8,1024]{2,1,0:T(8,128)(2,1)} copy(bf16[12,8,1024]{2,1,0:T(8,128)(2,1)} %bitcast.13) | data formatting | bytes 393216
  67.7 1.6 %copy.13 = bf16[12,8,1024]{2,1,0:T(8,128)(2,1)} copy(bf16[12,8,1024]{2,1,0:T(8,128)(2,1)} %bitcast.12) | data formatting | bytes 393216

commit v5 on v4

--- a/solution.py
+++ b/solution.py
@@ -263,6 +263,10 @@
 
     one, two, three = (1,), (2,), tuple(range(3, n_lat))
 
+    for a in range(2):
+        for way in (1, -1):
+            pl.when(onward(way, 1))(lambda: w1_copy(a, way, 1).start())
+
     for c in range(CHUNKS):
         @pl.when(has_up)
         def _():
@@ -277,10 +281,6 @@
         for a in range(2):
             for way in range(2):
                 lon_copy(a, 1, way, c).start()
-
-    for a in range(2):
-        for way in (1, -1):
-            pl.when(onward(way, 1))(lambda: w1_copy(a, way, 1).start())
 
     pad_rows = kbuf.shape[0] - 3 * seg
     for ref in (kbuf, vbuf):
@@ -395,132 +395,59 @@
         lo[:, at] = two_heads(q_ref[:, at], kbuf[:, at], vbuf[:, at], fix)
 
     per = cw // 128
+    spread(0, one)
+    spread(1, one)
     forward(0)
+    forward(1)
     own_copies[5].wait()
     for copy in own_copies[:2]:
         copy.wait()
-    forward(1)
-    forward(2)
     for c in range(CHUNKS):
         landed(c)
         pl.loop(c * per, (c + 1) * per, unroll=per)(local_pair)
         if c == 0:
+            forward(2)
+            spread(0, two)
+            spread(1, two)
+            relay(0, one)
+        if c == 1:
             forward(3)
-            spread(0, one)
-        if c == 1:
-            spread(0, two)
-            relay(0, one)
-            spread(1, one)
+            spread(0, three)
+            spread(1, three)
+            relay(1, one)
+            relay(0, two)
         if c == 2:
-            spread(0, three)
-            relay(0, two)
-            spread(1, two)
             corner(0, one)
-    relay(0, three)
-    corner(0, two)
+            relay(1, two)
+            relay(0, three)
+            corner(0, two)
+            corner(1, one)
     corner(0, three)
-    relay(1, one)
     own_copies[6].wait()
     own_copies[7].wait()
     gathered(0)
 
-    projected = jnp.dot(lo[...], wo[...], preferred_element_type=jnp.float32)
-    hidden = (tok_ref[...].astype(jnp.float32) + projected).astype(jnp.bfloat16)
-    hid_ref[...] = hidden
-    wide = hidden.astype(jnp.float32)
-    inverse = lax.rsqrt(jnp.mean(wide * wide, axis=1, keepdims=True) + 1e-06)
-    nbuf[pl.ds(0, tokens), :] = (wide * inverse * gain_ref[...]).astype(jnp.bfloat16)
-
-    def block(s):
-        return nbuf.at[pl.ds(s * tokens, tokens)]
-
-    def ex_copy(s):
-        return rc(block(0), block(s), ex_s.at[s], ex_r.at[s], line_dev(s))
-
-    staged = n_lat == 4
-
-    def direct(s, act):
-        if staged and s == 3:
-            pl.when(z != 0)(act)
-        elif staged and s == 1:
-            pl.when(z != n_lat - 1)(act)
-        else:
-            act()
-
-    up_copy = rc(block(2), block(3), ex_s.at[0], ex_r.at[3], lat_dev(1))
-    down_copy = rc(block(2), block(1), ex_s.at[0], ex_r.at[1], lat_dev(-1))
-
-    for s in (2, 3, 1, 4):
-        direct(s, lambda: ex_copy(s).start())
-    spread(1, three)
-    relay(1, two)
-    corner(1, one)
-    ex_copy(2).wait_recv()
-    if staged:
-        pl.when(z == 2)(lambda: up_copy.start())
-        pl.when(z == 1)(lambda: down_copy.start())
-    relay(1, three)
-    corner(1, two)
-    corner(1, three)
-    gathered(1)
-
-    tile = 512
-
-    def project(at, count, column):
-        left_rows = nbuf[pl.ds(at, count), :]
-        weight = wg[:, pl.ds(pl.multiple_of(column, tile), tile)]
-        return jnp.dot(left_rows, weight, preferred_element_type=jnp.float32).astype(jnp.bfloat16)
-
-    def keys_values(at, count):
-        @pl.loop(0, width // tile)
-        def _(t):
-            here = pl.ds(pl.multiple_of(t * tile, tile), tile)
-            gk[pl.ds(at, count), here] = project(at, count, width + t * tile)
-            gv[pl.ds(at, count), here] = project(at, count, 2 * width + t * tile)
-
-    @pl.loop(0, width // tile)
-    def _(t):
-        here = pl.ds(pl.multiple_of(t * tile, tile), tile)
-        gq[:, here] = project(0, tokens, t * tile)
-
-    for s in (1, 3, 4):
-        ex_copy(s).wait_recv()
-    keys_values(0, (STEPS + 1) * tokens)
-
-    def global_pair(h):
-        at = pl.ds(pl.multiple_of(h * 128, 128), 128)
-
-        def fix(s):
-            edge = s.shape[1] - 128
-            last = s[:, edge:]
-            key = lax.broadcasted_iota(jnp.int32, last.shape, 1)
-            last = jnp.where(key < (STEPS + 1) * tokens - edge, last, NEG)
-            return jnp.concatenate([s[:, :edge], last], axis=1)
-
-        att_ref[:, at] = two_heads(gq[:, at], gk[:, at], gv[:, at], fix)
-
-    pl.loop(0, width // 128, unroll=4)(global_pair)
-
-    for c in range(CHUNKS):
-        for a in range(2):
-            for way in range(2):
-                lon_copy(a, 1, way, c).wait_send()
-
-        @pl.when(has_up)
-        def _():
+    def halo_sent():
+        for c in range(CHUNKS):
             for a in range(2):
-                lat_copy(a, 0, c).wait_send()
                 for way in range(2):
-                    lon_copy(a, 2, way, c).wait_send()
-
-        @pl.when(has_down)
-        def _():
-            for a in range(2):
-                lat_copy(a, 1, c).wait_send()
-                for way in range(2):
-                    lon_copy(a, 0, way, c).wait_send()
-
-    for a in range(2):
+                    lon_copy(a, 1, way, c).wait_send()
+
+            @pl.when(has_up)
+            def _():
+                for a in range(2):
+                    lat_copy(a, 0, c).wait_send()
+                    for way in range(2):
+                        lon_copy(a, 2, way, c).wait_send()
+
+            @pl.when(has_down)
+            def _():
+                for a in range(2):
+                    lat_copy(a, 1, c).wait_send()
+                    for way in range(2):
+                        lon_copy(a, 0, way, c).wait_send()
+
+    def weights_sent(a):
         def sent(way, d):
             t = shard_of(way, d)
             wp_copy(a, t, j).wait_send()
@@ -534,6 +461,83 @@
         each(range(1, n_lat), sent)
         for way, d in routes:
             pl.when(onward(way, d))(lambda: w1_copy(a, way, d).wait_send())
+    projected = jnp.dot(lo[...], wo[...], preferred_element_type=jnp.float32)
+    hidden = (tok_ref[...].astype(jnp.float32) + projected).astype(jnp.bfloat16)
+    hid_ref[...] = hidden
+    wide = hidden.astype(jnp.float32)
+    inverse = lax.rsqrt(jnp.mean(wide * wide, axis=1, keepdims=True) + 1e-06)
+    nbuf[pl.ds(0, tokens), :] = (wide * inverse * gain_ref[...]).astype(jnp.bfloat16)
+
+    def block(s):
+        return nbuf.at[pl.ds(s * tokens, tokens)]
+
+    def ex_copy(s):
+        return rc(block(0), block(s), ex_s.at[s], ex_r.at[s], line_dev(s))
+
+    staged = n_lat == 4
+
+    def direct(s, act):
+        if staged and s == 3:
+            pl.when(z != 0)(act)
+        elif staged and s == 1:
+            pl.when(z != n_lat - 1)(act)
+        else:
+            act()
+
+    up_copy = rc(block(2), block(3), ex_s.at[0], ex_r.at[3], lat_dev(1))
+    down_copy = rc(block(2), block(1), ex_s.at[0], ex_r.at[1], lat_dev(-1))
+
+    for s in (2, 3, 1, 4):
+        direct(s, lambda: ex_copy(s).start())
+    relay(1, three)
+    corner(1, two)
+    halo_sent()
+    weights_sent(0)
+    ex_copy(2).wait_recv()
+    if staged:
+        pl.when(z == 2)(lambda: up_copy.start())
+        pl.when(z == 1)(lambda: down_copy.start())
+    corner(1, three)
+    gathered(1)
+
+    tile = 512
+
+    def project(at, count, column):
+        left_rows = nbuf[pl.ds(at, count), :]
+        weight = wg[:, pl.ds(pl.multiple_of(column, tile), tile)]
+        return jnp.dot(left_rows, weight, preferred_element_type=jnp.float32).astype(jnp.bfloat16)
+
+    def keys_values(at, count):
+        @pl.loop(0, width // tile)
+        def _(t):
+            here = pl.ds(pl.multiple_of(t * tile, tile), tile)
+            gk[pl.ds(at, count), here] = project(at, count, width + t * tile)
+            gv[pl.ds(at, count), here] = project(at, count, 2 * width + t * tile)
+
+    @pl.loop(0, width // tile)
+    def _(t):
+        here = pl.ds(pl.multiple_of(t * tile, tile), tile)
+        gq[:, here] = project(0, tokens, t * tile)
+
+    for s in (1, 3, 4):
+        ex_copy(s).wait_recv()
+    keys_values(0, (STEPS + 1) * tokens)
+
+    def global_pair(h):
+        at = pl.ds(pl.multiple_of(h * 128, 128), 128)
+
+        def fix(s):
+            edge = s.shape[1] - 128
+            last = s[:, edge:]
+            key = lax.broadcasted_iota(jnp.int32, last.shape, 1)
+            last = jnp.where(key < (STEPS + 1) * tokens - edge, last, NEG)
+            return jnp.concatenate([s[:, :edge], last], axis=1)
+
+        att_ref[:, at] = two_heads(gq[:, at], gk[:, at], gv[:, at], fix)
+
+    pl.loop(0, width // 128, unroll=4)(global_pair)
+
+    weights_sent(1)
     for s in range(1, STEPS + 1):
         direct(s, lambda: ex_copy(s).wait_send())
     if staged:

time: 69.5 us -> 73.3 us (1.055)
  Pallas kernels: 65.5 us -> 69.2 us
    pallas_call x1, Pallas kernels: 65.5 us -> 69.2 us  [body(): pl.pallas_call(functools.partial(kernel, n_lon, n_lat, pieces), out_shape...]
where the time goes in v5:
time: 73.3 us; the launch traced here: 73.1 us
  Pallas kernels  69.2 us (94%)
  local copies, waits for them, and re-layouts  3.23 us (4%)
    pallas_call x1, Pallas kernels, body(): pl.pallas_call(functools.partial(kernel, n_lon, n_lat, pieces), out_shape...  69.2 us
    unnamed x2, local copies, waits for them, and re-layouts  3.23 us

profile of v5, /device:TPU:0, one launch (start us, length us, event | category | flops | bytes accessed | tf_op | source)
XLA Modules:
  0.0 73.1 jit_solution(11786300219225800609)
XLA Ops:
  0.6 69.2 %shard_map.95 = (bf16[96,1024]{1,0:T(8,128)(2,1)}, bf16[96,1024]{1,0:T(8,128)(2,1)}) custom-call(bf16[96,1024]{1,0:T(8,128)(2,1)} %bitcast.8, bf16[96,1024]{1,0:T(8,128)(2,1)} %bitcast.9, bf16[96,1024]{1,0:T(8,128)(2,1)} %bitcast.10, bf16[96,1024]{1,0:T(8,128)(2,1)} %bitcast.11, f32[13,16,13]{2,1,0:T(8,128)} %bitcast.14, bf16[256,1024]{1,0:T(8,128)(2,1)} %wo_hbm.1, ...), custom_call_target="tpu_custom_call" | custom-call | tf_op jit(solution)/shard_map/pallas_call | solution.py:566
  69.9 1.6 %copy.12 = bf16[12,8,1024]{2,1,0:T(8,128)(2,1)} copy(bf16[12,8,1024]{2,1,0:T(8,128)(2,1)} %bitcast.13) | data formatting | bytes 393216
  71.5 1.6 %copy.13 = bf16[12,8,1024]{2,1,0:T(8,128)(2,1)} copy(bf16[12,8,1024]{2,1,0:T(8,128)(2,1)} %bitcast.12) | data formatting | bytes 393216

commit v6 on v5

--- a/solution.py
+++ b/solution.py
@@ -263,24 +263,24 @@
 
     one, two, three = (1,), (2,), tuple(range(3, n_lat))
 
+    for c in range(CHUNKS):
+        @pl.when(has_up)
+        def _():
+            for a in range(2):
+                lat_copy(a, 0, c).start()
+
+        @pl.when(has_down)
+        def _():
+            for a in range(2):
+                lat_copy(a, 1, c).start()
+
+        for a in range(2):
+            for way in range(2):
+                lon_copy(a, 1, way, c).start()
+
     for a in range(2):
         for way in (1, -1):
             pl.when(onward(way, 1))(lambda: w1_copy(a, way, 1).start())
-
-    for c in range(CHUNKS):
-        @pl.when(has_up)
-        def _():
-            for a in range(2):
-                lat_copy(a, 0, c).start()
-
-        @pl.when(has_down)
-        def _():
-            for a in range(2):
-                lat_copy(a, 1, c).start()
-
-        for a in range(2):
-            for way in range(2):
-                lon_copy(a, 1, way, c).start()
 
     pad_rows = kbuf.shape[0] - 3 * seg
     for ref in (kbuf, vbuf):
@@ -395,34 +395,31 @@
         lo[:, at] = two_heads(q_ref[:, at], kbuf[:, at], vbuf[:, at], fix)
 
     per = cw // 128
-    spread(0, one)
-    spread(1, one)
     forward(0)
-    forward(1)
     own_copies[5].wait()
     for copy in own_copies[:2]:
         copy.wait()
+    forward(1)
+    forward(2)
     for c in range(CHUNKS):
         landed(c)
         pl.loop(c * per, (c + 1) * per, unroll=per)(local_pair)
         if c == 0:
-            forward(2)
+            forward(3)
+            spread(0, one)
+        if c == 1:
             spread(0, two)
+            relay(0, one)
+            spread(1, one)
+        if c == 2:
+            spread(0, three)
+            relay(0, two)
             spread(1, two)
-            relay(0, one)
-        if c == 1:
-            forward(3)
-            spread(0, three)
-            spread(1, three)
-            relay(1, one)
-            relay(0, two)
-        if c == 2:
             corner(0, one)
-            relay(1, two)
-            relay(0, three)
-            corner(0, two)
-            corner(1, one)
+    relay(0, three)
+    corner(0, two)
     corner(0, three)
+    relay(1, one)
     own_copies[6].wait()
     own_copies[7].wait()
     gathered(0)
@@ -461,6 +458,7 @@
         each(range(1, n_lat), sent)
         for way, d in routes:
             pl.when(onward(way, d))(lambda: w1_copy(a, way, d).wait_send())
+
     projected = jnp.dot(lo[...], wo[...], preferred_element_type=jnp.float32)
     hidden = (tok_ref[...].astype(jnp.float32) + projected).astype(jnp.bfloat16)
     hid_ref[...] = hidden
@@ -489,14 +487,17 @@
 
     for s in (2, 3, 1, 4):
         direct(s, lambda: ex_copy(s).start())
+    spread(1, three)
+    relay(1, two)
+    corner(1, one)
+    ex_copy(2).wait_recv()
+    if staged:
+        pl.when(z == 2)(lambda: up_copy.start())
+        pl.when(z == 1)(lambda: down_copy.start())
     relay(1, three)
     corner(1, two)
     halo_sent()
     weights_sent(0)
-    ex_copy(2).wait_recv()
-    if staged:
-        pl.when(z == 2)(lambda: up_copy.start())
-        pl.when(z == 1)(lambda: down_copy.start())
     corner(1, three)
     gathered(1)
 
@@ -519,9 +520,10 @@
         here = pl.ds(pl.multiple_of(t * tile, tile), tile)
         gq[:, here] = project(0, tokens, t * tile)
 
+    keys_values(0, tokens)
     for s in (1, 3, 4):
         ex_copy(s).wait_recv()
-    keys_values(0, (STEPS + 1) * tokens)
+    keys_values(tokens, STEPS * tokens)
 
     def global_pair(h):
         at = pl.ds(pl.multiple_of(h * 128, 128), 128)

time: 73.3 us -> 69.9 us (0.954)
  Pallas kernels: 69.2 us -> 65.9 us
    pallas_call x1, Pallas kernels: 69.2 us -> 65.9 us  [body(): pl.pallas_call(functools.partial(kernel, n_lon, n_lat, pieces), out_shape...]
where the time goes in v6:
time: 69.9 us; the launch traced here: 69.8 us
  Pallas kernels  65.9 us (94%)
  local copies, waits for them, and re-layouts  3.23 us (5%)
    pallas_call x1, Pallas kernels, body(): pl.pallas_call(functools.partial(kernel, n_lon, n_lat, pieces), out_shape...  65.9 us
    unnamed x2, local copies, waits for them, and re-layouts  3.23 us

profile of v6, /device:TPU:0, one launch (start us, length us, event | category | flops | bytes accessed | tf_op | source)
XLA Modules:
  0.0 69.8 jit_solution(14825259033585518440)
XLA Ops:
  0.6 65.9 %shard_map.95 = (bf16[96,1024]{1,0:T(8,128)(2,1)}, bf16[96,1024]{1,0:T(8,128)(2,1)}) custom-call(bf16[96,1024]{1,0:T(8,128)(2,1)} %bitcast.8, bf16[96,1024]{1,0:T(8,128)(2,1)} %bitcast.9, bf16[96,1024]{1,0:T(8,128)(2,1)} %bitcast.10, bf16[96,1024]{1,0:T(8,128)(2,1)} %bitcast.11, f32[13,16,13]{2,1,0:T(8,128)} %bitcast.14, bf16[256,1024]{1,0:T(8,128)(2,1)} %wo_hbm.1, ...), custom_call_target="tpu_custom_call" | custom-call | tf_op jit(solution)/shard_map/pallas_call | solution.py:568
  66.5 1.6 %copy.12 = bf16[12,8,1024]{2,1,0:T(8,128)(2,1)} copy(bf16[12,8,1024]{2,1,0:T(8,128)(2,1)} %bitcast.13) | data formatting | bytes 393216
  68.2 1.6 %copy.13 = bf16[12,8,1024]{2,1,0:T(8,128)(2,1)} copy(bf16[12,8,1024]{2,1,0:T(8,128)(2,1)} %bitcast.12) | data formatting | bytes 393216
